TPU v7x, 32 devices: a whole 2x2x4 slice. The times are simulated.
32 devices in a mesh: lat: 8 (over z, y), lon: 4 (over x, core).
Axes of the slice: x: 2, y: 2, z: 4, core: 2. Of those that a mesh axis runs over, the one named last changes fastest.
Arguments:
- initial_state: float32 [6, 384, 512], P(None, 'lat', 'lon'), may hold values from -6 to 6
- source: float32 [6, 384, 512], P(None, 'lat', 'lon'), may hold values from -3 to 3
- cotangent: float32 [6, 384, 512], P(None, 'lat', 'lon'), may hold values from -6 to 6
- face_coefs: float32 [2, 384, 512], P(None, 'lat', 'lon'), may hold values from 0.03 to 0.1
- land_mask: int32 [6, 384, 512], P(None, 'lat', 'lon'), may hold values 0 or 1
- bottom: int32 [384, 512], P('lat', 'lon'), may hold values from 1 to 6
Outputs:
- final_state: float32 [6, 384, 512], P(None, 'lat', 'lon')
- grad_initial: float32 [6, 384, 512], P(None, 'lat', 'lon')
- grad_source: float32 [6, 384, 512], P(None, 'lat', 'lon')
All inputs are finite; a program needn't handle non-finite values. No bound on the sum of `land_mask` on one device may be relied on, other than what follows from the above.
Results may differ from a plain program's by a relative error of at most 0.00002.
Values sent between devices are 32-bit elements; how exact they have to be, the bound alone decides.
No kernel may reach another device: no remote copies, remote signals or barrier semaphores. Data moves between devices by JAX's collectives and lax.ppermute only.
A program may use at most 64 MiB of HBM per device.

v0:
```python
import functools

import jax
import jax.numpy as jnp
from jax import lax
from jax.experimental import pallas as pl
from jax.experimental.pallas import tpu as pltpu
from jax.sharding import PartitionSpec as P

STEPS = 4
DEPTH = 2 * STEPS
TILE = 8
HALO = TILE

vertical_coef = 0.04


class Names:
    def __init__(self, levels):
        self.levels = levels
        self.u, self.s, self.wet = 0, levels, 2 * levels
        self.ce, self.cn, self.cot = 3 * levels, 3 * levels + 1, 3 * levels + 2
        self.count = 4 * levels + 2
        self.parts = -(-self.count // 16)
        self.strips = 2 * self.parts
        self.first = self.ce
        self.cot_at = self.strips + 2
        self.second = self.cot_at + -(-levels // 2)


def lane_iota(lanes):
    return lax.broadcasted_iota(jnp.int32, (TILE, lanes), 1)


def shift_of(channel):
    place = channel % 16
    return 2 * DEPTH * (place % 8) + DEPTH * (place // 8)


def even_groups(lanes):
    return lax.rem(lane_iota(lanes) // DEPTH, 2) == 0


def is_odd(axis):
    return lax.rem(lax.axis_index(axis), 2) == 1


def strip_rows(c, m):
    return range(16 * m, min(16 * m + 16, c.count))


def pack_kernel(
    c, u_hbm, s_hbm, a_hbm, c_hbm, land_hbm, bottom_hbm, f_ref, first_ref, second_ref, lat_one_ref, lat_two_ref,
    u_ref, s_ref, c_ref, land_ref, bottom_ref, sems,
):
    levels = c.levels
    _, rows, lanes = u_ref.shape
    moves = [
        pltpu.make_async_copy(source, target, sems.at[i])
        for i, (source, target) in enumerate(
            (
                (bottom_hbm, bottom_ref),
                (land_hbm, land_ref),
                (u_hbm, u_ref),
                (s_hbm, s_ref),
                (c_hbm, c_ref),
                (a_hbm, f_ref.at[pl.ds(c.cot, levels)]),
            )
        )
    ]
    for move in moves:
        move.start()
    for move in moves:
        move.wait()
    last_lat = lax.axis_index("lat") == lax.axis_size("lat") - 1
    for k in range(levels):
        wet = jnp.where(k < bottom_ref[...], land_ref[k], 0).astype(jnp.float32)
        f_ref[c.u + k] = wet * u_ref[k]
        f_ref[c.s + k] = wet * s_ref[k]
        f_ref[c.wet + k] = wet
    f_ref[c.ce] = c_ref[0]
    row = lax.broadcasted_iota(jnp.int32, (rows, lanes), 0)
    f_ref[c.cn] = jnp.where(jnp.logical_and(last_lat, row == rows - 1), 0.0, c_ref[1])
    odd = is_odd("lon")
    group, groups = lane_iota(lanes) // DEPTH, lanes // DEPTH
    for t in range(rows // TILE):
        at = pl.ds(t * TILE, TILE)
        for m in range(c.parts):
            east = jnp.zeros((TILE, lanes), jnp.float32)
            west = east
            for channel in strip_rows(c, m):
                shift = shift_of(channel)
                tile = f_ref[channel, at, :]
                if shift:
                    tile = pltpu.roll(tile, shift, 1)
                east = jnp.where(group == shift // DEPTH, tile, east)
                west = jnp.where(group == (shift // DEPTH - 1) % groups, tile, west)
            first_ref[m, at, :] = jnp.where(odd, east, west)
            second_ref[m, at, :] = jnp.where(odd, west, east)
    odd_lat = is_odd("lat")
    for channel in range(c.first):
        high, low = f_ref[channel, pl.ds(rows - TILE, TILE), :], f_ref[channel, pl.ds(0, TILE), :]
        lat_one_ref[channel] = jnp.where(odd_lat, low, high)
        lat_two_ref[channel] = jnp.where(odd_lat, high, low)


def corner_kernel(c, f_ref, one_ref, two_ref, lat_one_ref, lat_two_ref):
    odd_lat, odd_lon = is_odd("lat"), is_odd("lon")
    _, rows, lanes = f_ref.shape
    half = TILE // 2
    first_half = lax.broadcasted_iota(jnp.int32, (TILE, lanes), 0) < half
    low, high = pl.ds(0, TILE), pl.ds(rows - TILE, TILE)

    def put(i, low_tile, high_tile):
        lat_one_ref[i] = jnp.where(odd_lat, low_tile, high_tile)
        lat_two_ref[i] = jnp.where(odd_lat, high_tile, low_tile)

    for m in range(c.parts):
        ends = [(one_ref[m, at, :], two_ref[m, at, :]) for at in (low, high)]
        put(m, *(jnp.where(odd_lon, two, one) for one, two in ends))
        put(c.parts + m, *(jnp.where(odd_lon, one, two) for one, two in ends))
    put(c.strips, f_ref[c.ce, low, :], f_ref[c.ce, high, :])
    put(c.strips + 1, f_ref[c.cn, low, :], f_ref[c.cn, high, :])
    for q in range(c.second - c.cot_at):
        one, two = c.cot + 2 * q, c.cot + min(2 * q + 1, c.levels - 1)
        put(
            c.cot_at + q,
            jnp.where(first_half, f_ref[one, low, :], pltpu.roll(f_ref[two, low, :], half, 0)),
            jnp.where(first_half, pltpu.roll(f_ref[one, high, :], half, 0), f_ref[two, high, :]),
        )


class Sweeps:
    def __init__(self, c, e, w, d, x, m, adj, state):
        self.c, self.e, self.w, self.d, self.x, self.m, self.adj, self.state = c, e, w, d, x, m, adj, state
        self.lanes = e[0].shape[-1]
        lane = lane_iota(self.lanes)
        self.at_first, self.at_last = lane == 0, lane == self.lanes - 1
        self.even_group = even_groups(self.lanes)

    def from_west(self, x0, x1):
        r0, r1 = pltpu.roll(x0, 1, 1), pltpu.roll(x1, 1, 1)
        return jnp.where(self.at_first, r1, r0), jnp.where(self.at_first, r0, r1)

    def from_east(self, x0, x1):
        r0, r1 = pltpu.roll(x0, self.lanes - 1, 1), pltpu.roll(x1, self.lanes - 1, 1)
        return jnp.where(self.at_last, r1, r0), jnp.where(self.at_last, r0, r1)

    def spread(self, row, easts, wests):
        for m, (east, west) in enumerate(zip(easts, wests)):
            both = jnp.where(self.even_group, east, west), jnp.where(self.even_group, west, east)
            for channel in strip_rows(self.c, m):
                shift = shift_of(channel)
                tile = both[(channel % 16) // 8]
                if shift:
                    tile = pltpu.roll(tile, self.lanes - shift, 1)
                self.e[1][channel, pl.ds(row, TILE), :] = tile

    def western(self, row):
        at = pl.ds(row, TILE)
        self.w[0][at, :], self.w[1][at, :] = self.from_west(self.e[0][self.c.ce, at, :], self.e[1][self.c.ce, at, :])

    def neighbours(self, load, row, halves=2):
        c, at = self.c, pl.ds(row, TILE)
        ce = [e[c.ce, at, :] for e in self.e]
        cw = [w[at, :] for w in self.w]
        cn = [e[c.cn, at, :] for e in self.e]
        cs = [e[c.cn, pl.ds(row - 1, TILE), :] for e in self.e]
        own = [(load(0, k, at), load(1, k, at)) for k in range(c.levels)]
        out = []
        for k in range(c.levels):
            east, west = self.from_east(*own[k]), self.from_west(*own[k])
            pair = []
            for h in range(halves):
                north, south = load(h, k, pl.ds(row + 1, TILE)), load(h, k, pl.ds(row - 1, TILE))
                total = (ce[h] * east[h] + cw[h] * west[h]) + (cn[h] * north + cs[h] * south)
                around = [own[j][h] for j in (k - 1, k + 1) if 0 <= j < c.levels]
                pair.append((own[k][h], total + vertical_coef * functools.reduce(jnp.add, around)))
            out.append(pair)
        return out

    def diagonal(self, row):
        load = lambda h, k, at: self.e[h][self.c.wet + k, at, :]
        for k, pair in enumerate(self.neighbours(load, row)):
            for h, (_, total) in enumerate(pair):
                self.d[h][k, pl.ds(row, TILE), :] = 1.0 - total

    def loader(self, index):
        if index == 0:
            return lambda h, k, at: self.e[h][self.c.u + k, at, :]
        base = (index - 1) * self.c.levels
        return lambda h, k, at: self.x[h][base + k, at, :]

    def forward(self, n, row):
        c, at = self.c, pl.ds(row, TILE)
        for k, pair in enumerate(self.neighbours(self.loader(n), row)):
            for h, (own, total) in enumerate(pair):
                e = self.e[h]
                wet = e[c.wet + k, at, :]
                bounded = wet * jnp.tanh(self.d[h][k, at, :] * own + total)
                slope = wet - bounded * bounded
                if n < STEPS - 1:
                    self.x[h][n * c.levels + k, at, :] = bounded + e[c.s + k, at, :]
                    self.m[h][n * c.levels + k, at, :] = slope
                else:
                    if h == 0:
                        self.state[k, at, :] = bounded + e[c.s + k, at, :]
                    self.x[h][n * c.levels + k, at, :] = slope * e[c.cot + k, at, :]

    def backward(self, n, row):
        c, at = self.c, pl.ds(row, TILE)
        index = 2 * STEPS - 1 - n
        for k, pair in enumerate(self.neighbours(self.loader(index), row)):
            for h, (own, total) in enumerate(pair):
                value = self.d[h][k, at, :] * own + total
                if h == 0:
                    self.adj[(n - 1) * c.levels + k, at, :] = value
                self.x[h][index * c.levels + k, at, :] = self.m[h][(n - 1) * c.levels + k, at, :] * value

    def gradient(self, row):
        c, at = self.c, pl.ds(row, TILE)
        for k, pair in enumerate(self.neighbours(self.loader(2 * STEPS - 1), row, 1)):
            own, total = pair[0]
            yield k, self.e[0][c.wet + k, at, :] * (self.d[0][k, at, :] * own + total)

    def source_gradient(self, row):
        c, at = self.c, pl.ds(row, TILE)
        for k in range(c.levels):
            total = self.e[0][c.cot + k, at, :]
            for n in range(STEPS - 1):
                total = total + self.adj[n * c.levels + k, at, :]
            yield k, self.e[0][c.wet + k, at, :] * total


def own_kernel(c, f_ref, one_ref, two_ref, e0, e1, w0, w1, d0, d1, x0, x1, m0, m1, adj, state, grad, gsource):
    rows = f_ref.shape[1]
    odd_lon = is_odd("lon")
    s = Sweeps(c, (e0, e1), (w0, w1), (d0, d1), (x0, x1), (m0, m1), adj, state)
    zero = jnp.zeros((TILE, f_ref.shape[2]), jnp.float32)
    for ref in (e0, e1):
        for end in (pl.ds(0, TILE), pl.ds(HALO + rows, TILE)):
            for channel in (*range(c.u, c.u + c.levels), *range(c.wet, c.wet + c.levels), c.cn):
                ref[channel, end, :] = zero
    tiles = rows // TILE
    places = [HALO + t * TILE for t in range(tiles)]
    for t, row in enumerate(places):
        at, to = pl.ds(t * TILE, TILE), pl.ds(row, TILE)
        for channel in range(c.count):
            e0[channel, to, :] = f_ref[channel, at, :]
        pairs = [(one_ref[m, at, :], two_ref[m, at, :]) for m in range(c.parts)]
        s.spread(
            row,
            [jnp.where(odd_lon, two, one) for one, two in pairs],
            [jnp.where(odd_lon, one, two) for one, two in pairs],
        )
        s.western(row)
    for row in places:
        s.diagonal(row)
    for n in range(STEPS):
        for row in places:
            s.forward(n, row)
    for n in range(STEPS - 1, 0, -1):
        for row in places:
            s.backward(n, row)
    for row in places[1:-1]:
        at = pl.ds(row - HALO, TILE)
        for k, value in s.source_gradient(row):
            gsource[k, at, :] = value
        for k, value in s.gradient(row):
            grad[k, at, :] = value


def edge_kernel(
    c, first_one, first_two, second_two, second_one, *refs,
):
    aliased = refs[: len(refs) // 2]
    del aliased
    e0, e1, w0, w1, d0, d1, x0, x1, m0, m1, adj, state, grad, gsource, state_hbm, grad_hbm, gsource_hbm, sems = refs[14:]
    rows = grad.shape[1]
    s = Sweeps(c, (e0, e1), (w0, w1), (d0, d1), (x0, x1), (m0, m1), adj, state)
    odd_lat = is_odd("lat")
    for row, low in ((0, True), (HALO + rows, False)):
        pole = lax.axis_index("lat") == (0 if low else lax.axis_size("lat") - 1)
        from_one = odd_lat if low else jnp.logical_not(odd_lat)
        to = pl.ds(row, TILE)

        def got(one, two, i):
            return jnp.where(pole, 0.0, jnp.where(from_one, one[i], two[i]))

        second = [got(second_one, second_two, i) for i in range(c.second)]
        for channel in range(c.first):
            e0[channel, to, :] = got(first_one, first_two, channel)
        e0[c.ce, to, :], e0[c.cn, to, :] = second[c.strips : c.cot_at]
        for k in range(c.levels):
            tile = second[c.cot_at + k // 2]
            if (k % 2 == 0) == low:
                tile = pltpu.roll(tile, TILE // 2, 0)
            e0[c.cot + k, to, :] = tile
        s.spread(row, second[: c.parts], second[c.parts : c.strips])
        s.western(row)
    top = lambda i: HALO + i - (DEPTH - 1)
    bottom = lambda i: HALO + rows - 1 - i
    places = lambda i: (top(i), bottom(i))
    for row in places(0):
        s.diagonal(row)
    for n in range(STEPS):
        for row in places(n):
            s.forward(n, row)
    own = pl.ds(HALO, rows)
    moves = [
        pltpu.make_async_copy(state.at[:, own, :], state_hbm, sems.at[0]),
        pltpu.make_async_copy(gsource, gsource_hbm, sems.at[1]),
        pltpu.make_async_copy(grad, grad_hbm, sems.at[2]),
    ]
    moves[0].start()
    for n in range(STEPS - 1, 0, -1):
        for row in places(2 * STEPS - 1 - n):
            s.backward(n, row)
    for row in places(DEPTH - 1):
        for k, value in s.source_gradient(row):
            gsource[k, pl.ds(row - HALO, TILE), :] = value
    moves[1].start()
    for row in places(DEPTH - 1):
        for k, value in s.gradient(row):
            grad[k, pl.ds(row - HALO, TILE), :] = value
    moves[2].start()
    for move in moves:
        move.wait()


def swaps(count, offset):
    pairs = [(i, (i + 1) % count) for i in range(offset, count, 2)]
    return pairs + [(j, i) for i, j in pairs]


def lat_swaps(lat, lon, offset):
    pairs, alone = [], set(range(lat))
    for i in range(offset, lat - 1, 2):
        alone -= {i, i + 1}
        pairs += [(i * lon + j, (i + 1) * lon + j) for j in range(lon)]
    for i in sorted(alone):
        pairs += [(i * lon + j, i * lon + j + 1) for j in range(0, lon, 2)]
    return pairs + [(j, i) for i, j in pairs]


def body(initial_state, source, cotangent, face_coefs, land_mask, bottom):
    arguments = (initial_state, source, cotangent, face_coefs, land_mask, bottom)
    levels, rows, lanes = initial_state.shape
    c = Names(levels)
    span = rows + 2 * HALO
    f32 = lambda *shape: jax.ShapeDtypeStruct(shape, jnp.float32)
    vmem, hbm = pl.BlockSpec(memory_space=pltpu.VMEM), pl.BlockSpec(memory_space=pltpu.HBM)
    params = pltpu.CompilerParams(vmem_limit_bytes=8 * 1024 * 1024)

    fields, one, two, lat_one, lat_two = pl.pallas_call(
        functools.partial(pack_kernel, c),
        out_shape=(f32(c.count, rows, lanes), *(f32(c.parts, rows, lanes),) * 2, *(f32(c.first, TILE, lanes),) * 2),
        in_specs=[hbm] * 6,
        out_specs=(vmem,) * 5,
        scratch_shapes=[
            pltpu.VMEM((levels, rows, lanes), jnp.float32),
            pltpu.VMEM((levels, rows, lanes), jnp.float32),
            pltpu.VMEM((2, rows, lanes), jnp.float32),
            pltpu.VMEM((levels, rows, lanes), jnp.int32),
            pltpu.VMEM((rows, lanes), jnp.int32),
            pltpu.SemaphoreType.DMA((6,)),
        ],
        compiler_params=params,
        name="pack",
    )(*(pltpu.with_memory_space_constraint(x, pltpu.HBM) for x in arguments))
    lon, lat = lax.axis_size("lon"), lax.axis_size("lat")
    one = lax.ppermute(one, "lon", swaps(lon, 0))
    two = lax.ppermute(two, "lon", swaps(lon, 1))
    both = ("lat", "lon")
    lat_pairs, other_pairs = lat_swaps(lat, lon, 0), lat_swaps(lat, lon, 1)
    first = lax.ppermute(lat_one, both, lat_pairs), lax.ppermute(lat_two, both, other_pairs)
    lat_one, lat_two = pl.pallas_call(
        functools.partial(corner_kernel, c),
        out_shape=(f32(c.second, TILE, lanes),) * 2,
        in_specs=[vmem] * 3,
        out_specs=(vmem,) * 2,
        compiler_params=params,
        name="corners",
    )(fields, one, two)
    second = lax.ppermute(lat_one, both, lat_pairs), lax.ppermute(lat_two, both, other_pairs)
    twice = lambda *shape: (f32(*shape), f32(*shape))
    shapes = (
        *twice(c.count, span, lanes),
        *twice(span, lanes),
        *twice(levels, span, lanes),
        *twice((2 * STEPS - 1) * levels, span, lanes),
        *twice((STEPS - 1) * levels, span, lanes),
        f32((STEPS - 1) * levels, span, lanes),
        f32(levels, span, lanes),
        f32(levels, rows, lanes),
        f32(levels, rows, lanes),
    )
    own = pl.pallas_call(
        functools.partial(own_kernel, c),
        out_shape=shapes,
        in_specs=[vmem] * 3,
        out_specs=(vmem,) * len(shapes),
        compiler_params=params,
        cost_estimate=pl.CostEstimate(
            flops=2 * STEPS * levels * rows * lanes * 40, bytes_accessed=16 * 2**20, transcendentals=0
        ),
        name="own_rows",
    )(fields, one, two)
    out = pl.pallas_call(
        functools.partial(edge_kernel, c),
        out_shape=(*shapes, *(f32(levels, rows, lanes),) * 3),
        in_specs=[vmem] * (4 + len(shapes)),
        out_specs=(*(vmem,) * len(shapes), hbm, hbm, hbm),
        input_output_aliases={4 + i: i for i in range(len(shapes))},
        scratch_shapes=[pltpu.SemaphoreType.DMA((3,))],
        compiler_params=params,
        name="edge_rows",
    )(*first, *second[::-1], *own)
    return tuple(out[len(shapes) :])


def solution(mesh):
    block = P(None, "lat", "lon")
    return jax.shard_map(
        body,
        mesh=mesh,
        in_specs=(block, block, block, block, block, P("lat", "lon")),
        out_specs=(block, block, block),
        check_vma=False,
    )
```

profile of v0, /device:TPU:0, one launch (start us, length us, event | category | flops | bytes accessed | tf_op | source)
XLA Modules:
  0.0 14.1 jit_solution(6825305590267205348)
XLA Ops:
  0.6 1.4 %pack.1 = (f32[26,48,128]{2,1,0:T(8,128)S(1)}, f32[2,48,128]{2,1,0:T(8,128)S(1)}, f32[2,48,128]{2,1,0:T(8,128)S(1)}, f32[18,8,128]{2,1,0:T(8,128)S(1)}, f32[18,8,128]{2,1,0:T(8,128)S(1)}) custom-call(f32[6,48,128]{2,1,0:T(8,128)} %u_hbm.1, f32[6,48,128]{2,1,0:T(8,128)} %s_hbm.1, f32[6,48,128]{2,1,0:T(8,128)} %a_hbm.1, f32[2,48,128]{2,1,0:T(8,128)} %c_hbm.1, ...), custom_call_target="tpu_custom_call" | custom-call | tf_op jit(solution)/shard_map/pack/pallas_call | solution.py:355
  2.1 0.5 %collective-permute-start.2 = (f32[2,48,128]{2,1,0:T(8,128)S(1)}, f32[2,48,128]{2,1,0:T(8,128)S(1)}, u32[]{:S(2)}, u32[]{:S(2)}) collective-permute-start(f32[2,48,128]{2,1,0:T(8,128)S(1)} %get-tuple-element.30), channel_id=1, source_target_pairs={{0,1},{2,3},{1,0},{3,2},{4,5},{6,7},{5,4},{7,6},{8,9},{10,11},{9,8... | collective-permute-start | bytes 147464 | tf_op jit(solution)/shard_map/ppermute | solution.py:372
  2.6 2.6 %collective-permute-start.3 = (f32[2,48,128]{2,1,0:T(8,128)S(1)}, f32[2,48,128]{2,1,0:T(8,128)S(1)}, u32[]{:S(2)}, u32[]{:S(2)}) collective-permute-start(f32[2,48,128]{2,1,0:T(8,128)S(1)} %get-tuple-element.31), channel_id=1, source_target_pairs={{1,2},{3,0},{2,1},{0,3},{5,6},{7,4},{6,5},{4,7},{9,10},{11,8},{10,... | collective-permute-start | bytes 147464 | tf_op jit(solution)/shard_map/ppermute | solution.py:373
  5.2 1.5 %collective-permute-start = (f32[18,8,128]{2,1,0:T(8,128)S(1)}, f32[18,8,128]{2,1,0:T(8,128)S(1)}, u32[]{:S(2)}, u32[]{:S(2)}) collective-permute-start(f32[18,8,128]{2,1,0:T(8,128)S(1)} %get-tuple-element.27), channel_id=1, source_target_pairs={{0,4},{1,5},{2,6},{3,7},{8,12},{9,13},{10,14},{11,15},{16,20},{17,... | collective-permute-start | bytes 221192 | tf_op jit(solution)/shard_map/ppermute | solution.py:376
  6.7 0.0 collective-permute-start.1
  6.7 0.0 collective-permute-done.2.one_ref
  6.7 0.5 %collective-permute-done.3.two_ref = f32[2,48,128]{2,1,0:T(8,128)S(1)} collective-permute-done((f32[2,48,128]{2,1,0:T(8,128)S(1)}, f32[2,48,128]{2,1,0:T(8,128)S(1)}, u32[]{:S(2)}, u32[]{:S(2)}) %collective-permute-start.3) | collective-permute-done | bytes 49184 | tf_op jit(solution)/shard_map/ppermute | solution.py:373
  7.3 0.2 %collective-permute-start.4 = (f32[9,8,128]{2,1,0:T(8,128)S(1)}, f32[9,8,128]{2,1,0:T(8,128)S(1)}, u32[]{:S(2)}, u32[]{:S(2)}) collective-permute-start(f32[9,8,128]{2,1,0:T(8,128)S(1)} %get-tuple-element.32), channel_id=1, source_target_pairs={{4,8},{5,9},{6,10},{7,11},{12,16},{13,17},{14,18},{15,19},{20,24},... | collective-permute-start | bytes 110600 | tf_op jit(solution)/shard_map/ppermute | solution.py:385
  7.4 2.9 %collective-permute-start.5 = (f32[9,8,128]{2,1,0:T(8,128)S(1)}, f32[9,8,128]{2,1,0:T(8,128)S(1)}, u32[]{:S(2)}, u32[]{:S(2)}) collective-permute-start(f32[9,8,128]{2,1,0:T(8,128)S(1)} %get-tuple-element.33), channel_id=1, source_target_pairs={{0,4},{1,5},{2,6},{3,7},{8,12},{9,13},{10,14},{11,15},{16,20},{17,... | collective-permute-start | bytes 110600 | tf_op jit(solution)/shard_map/ppermute | solution.py:385
  10.3 2.0 %own_rows.1 = (f32[26,64,128]{2,1,0:T(8,128)S(1)}, f32[26,64,128]{2,1,0:T(8,128)S(1)}, f32[64,128]{1,0:T(8,128)S(1)}, f32[64,128]{1,0:T(8,128)S(1)}, f32[6,64,12...) custom-call(f32[26,48,128]{2,1,0:T(8,128)S(1)} %get-tuple-element.29, ...), custom_call_target="tpu_custom_call" | custom-call | flops 11796480 | bytes 16777216 | tf_op jit(solution)/shard_map/own_rows/pallas_call | solution.py:398
  12.3 0.0 collective-permute-done.first_one
  12.4 0.0 collective-permute-done.1.first_two
  12.4 0.0 collective-permute-done.4.second_two
  12.4 0.0 collective-permute-done.5.second_one
  12.4 1.8 %edge_rows.1 = (f32[26,64,128]{2,1,0:T(8,128)S(1)}, f32[26,64,128]{2,1,0:T(8,128)S(1)}, f32[64,128]{1,0:T(8,128)S(1)}, f32[64,128]{1,0:T(8,128)S(1)}, f32[6,64,1...) custom-call(f32[18,8,128]{2,1,0:T(8,128)S(1)} %collective-permute-do, ...), custom_call_target="tpu_custom_call", output_to_operand_aliasing={{0}: (4, {}), {1}: (5, {}), {2}: (6, {}), {3}: (7, {}), {4}... | custom-call | tf_op jit(solution)/shard_map/edge_rows/pallas_call | solution.py:409
  (1 shorter events, 0.0 us)
Async XLA Ops:
  2.1 4.7 %collective-permute-start.2 = (f32[2,48,128]{2,1,0:T(8,128)S(1)}, f32[2,48,128]{2,1,0:T(8,128)S(1)}, u32[]{:S(2)}, u32[]{:S(2)}) collective-permute-start(f32[2,48,128]{2,1,0:T(8,128)S(1)} %get-tuple-element.30), channel_id=1, source_target_pairs={{0,1},{2,3},{1,0},{3,2},{4,5},{6,7},{5,4},{7,6},{8,9},{10,11},{9,8... | collective-permute-start | bytes 147464 | tf_op jit(solution)/shard_map/ppermute | solution.py:372
  2.6 4.6 %collective-permute-start.3 = (f32[2,48,128]{2,1,0:T(8,128)S(1)}, f32[2,48,128]{2,1,0:T(8,128)S(1)}, u32[]{:S(2)}, u32[]{:S(2)}) collective-permute-start(f32[2,48,128]{2,1,0:T(8,128)S(1)} %get-tuple-element.31), channel_id=1, source_target_pairs={{1,2},{3,0},{2,1},{0,3},{5,6},{7,4},{6,5},{4,7},{9,10},{11,8},{10,... | collective-permute-start | bytes 147464 | tf_op jit(solution)/shard_map/ppermute | solution.py:373
  5.2 7.1 %collective-permute-start = (f32[18,8,128]{2,1,0:T(8,128)S(1)}, f32[18,8,128]{2,1,0:T(8,128)S(1)}, u32[]{:S(2)}, u32[]{:S(2)}) collective-permute-start(f32[18,8,128]{2,1,0:T(8,128)S(1)} %get-tuple-element.27), channel_id=1, source_target_pairs={{0,4},{1,5},{2,6},{3,7},{8,12},{9,13},{10,14},{11,15},{16,20},{17,... | collective-permute-start | bytes 221192 | tf_op jit(solution)/shard_map/ppermute | solution.py:376
  6.7 5.6 %collective-permute-start.1 = (f32[18,8,128]{2,1,0:T(8,128)S(1)}, f32[18,8,128]{2,1,0:T(8,128)S(1)}, u32[]{:S(2)}, u32[]{:S(2)}) collective-permute-start(f32[18,8,128]{2,1,0:T(8,128)S(1)} %get-tuple-element.28), channel_id=1, source_target_pairs={{4,8},{5,9},{6,10},{7,11},{12,16},{13,17},{14,18},{15,19},{20,24},... | collective-permute-start | bytes 221192 | tf_op jit(solution)/shard_map/ppermute | solution.py:376
  7.3 5.1 %collective-permute-start.4 = (f32[9,8,128]{2,1,0:T(8,128)S(1)}, f32[9,8,128]{2,1,0:T(8,128)S(1)}, u32[]{:S(2)}, u32[]{:S(2)}) collective-permute-start(f32[9,8,128]{2,1,0:T(8,128)S(1)} %get-tuple-element.32), channel_id=1, source_target_pairs={{4,8},{5,9},{6,10},{7,11},{12,16},{13,17},{14,18},{15,19},{20,24},... | collective-permute-start | bytes 110600 | tf_op jit(solution)/shard_map/ppermute | solution.py:385
  7.4 4.9 %collective-permute-start.5 = (f32[9,8,128]{2,1,0:T(8,128)S(1)}, f32[9,8,128]{2,1,0:T(8,128)S(1)}, u32[]{:S(2)}, u32[]{:S(2)}) collective-permute-start(f32[9,8,128]{2,1,0:T(8,128)S(1)} %get-tuple-element.33), channel_id=1, source_target_pairs={{0,4},{1,5},{2,6},{3,7},{8,12},{9,13},{10,14},{11,15},{16,20},{17,... | collective-permute-start | bytes 110600 | tf_op jit(solution)/shard_map/ppermute | solution.py:385
where the time goes:
time: 14.3 us; the launch traced here: 14.1 us
  starting transfers between devices  7.71 us (54%)
  Pallas kernels  5.23 us (37%)
  between operations  0.68 us (5%)
  waiting for transfers between devices  0.51 us (4%)
    ppermute x2, starting transfers between devices, body(): lax.ppermute(lat_one, both, lat_pairs)  4.4 us
    ppermute x1, starting transfers between devices, body(): two = lax.ppermute(two, 'lon', swaps(lon, 1))  2.61 us
    pallas_call x1, Pallas kernels, body(): pl.pallas_call(functools.partial(own_kernel, c), out_shape=shapes, in_spe...  2.03 us
    pallas_call x1, Pallas kernels, body(): pl.pallas_call(functools.partial(edge_kernel, c), out_shape=(*shapes, *(f...  1.75 us
    pallas_call x1, Pallas kernels, body(): pl.pallas_call(functools.partial(pack_kernel, c), out_shape=(f32(c.count,...  1.44 us
    ppermute x1, starting transfers between devices, body(): one = lax.ppermute(one, 'lon', swaps(lon, 0))  0.52 us
    ppermute x1, waiting for transfers between devices, body(): two = lax.ppermute(two, 'lon', swaps(lon, 1))  0.49 us
  transfers between devices with their start and end apart: 6, of which 1 were waited for; matrix products, arithmetic and copies ran while one was open for 0% of the time, Pallas kernels for 14%

commit v1 on v0

--- a/solution.py
+++ b/solution.py
@@ -23,9 +23,11 @@
         self.count = 4 * levels + 2
         self.parts = -(-self.count // 16)
         self.strips = 2 * self.parts
-        self.first = self.ce
-        self.cot_at = self.strips + 2
-        self.second = self.cot_at + -(-levels // 2)
+        self.strips_at = self.ce
+        self.faces_at = self.strips_at + self.strips
+        self.cot_at = self.faces_at + 2
+        self.late = self.cot_at + -(-levels // 2)
+        self.early = max(self.count, self.late + 1)
 
 
 def lane_iota(lanes):
@@ -50,7 +52,7 @@
 
 
 def pack_kernel(
-    c, u_hbm, s_hbm, a_hbm, c_hbm, land_hbm, bottom_hbm, f_ref, first_ref, second_ref, lat_one_ref, lat_two_ref,
+    c, u_hbm, s_hbm, a_hbm, c_hbm, land_hbm, bottom_hbm, f_ref, first_ref, second_ref, lat_ref,
     u_ref, s_ref, c_ref, land_ref, bottom_ref, sems,
 ):
     levels = c.levels
@@ -98,32 +100,36 @@
             first_ref[m, at, :] = jnp.where(odd, east, west)
             second_ref[m, at, :] = jnp.where(odd, west, east)
     odd_lat = is_odd("lat")
-    for channel in range(c.first):
+    for channel in range(c.count):
         high, low = f_ref[channel, pl.ds(rows - TILE, TILE), :], f_ref[channel, pl.ds(0, TILE), :]
-        lat_one_ref[channel] = jnp.where(odd_lat, low, high)
-        lat_two_ref[channel] = jnp.where(odd_lat, high, low)
-
-
-def corner_kernel(c, f_ref, one_ref, two_ref, lat_one_ref, lat_two_ref):
+        lat_ref[channel] = jnp.where(odd_lat, low, high)
+    for channel in range(c.count, c.early):
+        lat_ref[channel] = jnp.zeros((TILE, lanes), jnp.float32)
+
+
+def corner_kernel(c, f_ref, two_ref, one_ref, strips_ref, late_ref):
     odd_lat, odd_lon = is_odd("lat"), is_odd("lon")
     _, rows, lanes = f_ref.shape
     half = TILE // 2
     first_half = lax.broadcasted_iota(jnp.int32, (TILE, lanes), 0) < half
     low, high = pl.ds(0, TILE), pl.ds(rows - TILE, TILE)
 
-    def put(i, low_tile, high_tile):
-        lat_one_ref[i] = jnp.where(odd_lat, low_tile, high_tile)
-        lat_two_ref[i] = jnp.where(odd_lat, high_tile, low_tile)
+    def late(i, low_tile, high_tile):
+        late_ref[i] = jnp.where(odd_lat, high_tile, low_tile)
+
+    def strips(i, low_tile, high_tile):
+        strips_ref[i] = jnp.where(odd_lat, low_tile, high_tile)
+        late(c.strips_at + i, low_tile, high_tile)
 
     for m in range(c.parts):
         ends = [(one_ref[m, at, :], two_ref[m, at, :]) for at in (low, high)]
-        put(m, *(jnp.where(odd_lon, two, one) for one, two in ends))
-        put(c.parts + m, *(jnp.where(odd_lon, one, two) for one, two in ends))
-    put(c.strips, f_ref[c.ce, low, :], f_ref[c.ce, high, :])
-    put(c.strips + 1, f_ref[c.cn, low, :], f_ref[c.cn, high, :])
-    for q in range(c.second - c.cot_at):
+        strips(m, *(jnp.where(odd_lon, two, one) for one, two in ends))
+        strips(c.parts + m, *(jnp.where(odd_lon, one, two) for one, two in ends))
+    for i, channel in (*((i, i) for i in range(c.strips_at)), (c.faces_at, c.ce), (c.faces_at + 1, c.cn)):
+        late(i, f_ref[channel, low, :], f_ref[channel, high, :])
+    for q in range(c.late - c.cot_at):
         one, two = c.cot + 2 * q, c.cot + min(2 * q + 1, c.levels - 1)
-        put(
+        late(
             c.cot_at + q,
             jnp.where(first_half, f_ref[one, low, :], pltpu.roll(f_ref[two, low, :], half, 0)),
             jnp.where(first_half, pltpu.roll(f_ref[one, high, :], half, 0), f_ref[two, high, :]),
@@ -232,7 +238,7 @@
             yield k, self.e[0][c.wet + k, at, :] * total
 
 
-def own_kernel(c, f_ref, one_ref, two_ref, e0, e1, w0, w1, d0, d1, x0, x1, m0, m1, adj, state, grad, gsource):
+def own_kernel(c, f_ref, two_ref, one_ref, e0, e1, w0, w1, d0, d1, x0, x1, m0, m1, adj, state, grad, gsource):
     rows = f_ref.shape[1]
     odd_lon = is_odd("lon")
     s = Sweeps(c, (e0, e1), (w0, w1), (d0, d1), (x0, x1), (m0, m1), adj, state)
@@ -271,7 +277,7 @@
 
 
 def edge_kernel(
-    c, first_one, first_two, second_two, second_one, *refs,
+    c, late, early, early_strips, *refs,
 ):
     aliased = refs[: len(refs) // 2]
     del aliased
@@ -281,22 +287,23 @@
     odd_lat = is_odd("lat")
     for row, low in ((0, True), (HALO + rows, False)):
         pole = lax.axis_index("lat") == (0 if low else lax.axis_size("lat") - 1)
-        from_one = odd_lat if low else jnp.logical_not(odd_lat)
+        from_early = odd_lat if low else jnp.logical_not(odd_lat)
         to = pl.ds(row, TILE)
 
-        def got(one, two, i):
-            return jnp.where(pole, 0.0, jnp.where(from_one, one[i], two[i]))
-
-        second = [got(second_one, second_two, i) for i in range(c.second)]
-        for channel in range(c.first):
-            e0[channel, to, :] = got(first_one, first_two, channel)
-        e0[c.ce, to, :], e0[c.cn, to, :] = second[c.strips : c.cot_at]
+        def got(early_tile, late_tile):
+            return jnp.where(pole, 0.0, jnp.where(from_early, early_tile, late_tile))
+
+        for channel in range(c.strips_at):
+            e0[channel, to, :] = got(early[channel], late[channel])
+        e0[c.ce, to, :] = got(early[c.ce], late[c.faces_at])
+        e0[c.cn, to, :] = got(early[c.cn], late[c.faces_at + 1])
         for k in range(c.levels):
-            tile = second[c.cot_at + k // 2]
+            tile = late[c.cot_at + k // 2]
             if (k % 2 == 0) == low:
                 tile = pltpu.roll(tile, TILE // 2, 0)
-            e0[c.cot + k, to, :] = tile
-        s.spread(row, second[: c.parts], second[c.parts : c.strips])
+            e0[c.cot + k, to, :] = got(early[c.cot + k], tile)
+        strips = [got(early_strips[i], late[c.strips_at + i]) for i in range(c.strips)]
+        s.spread(row, strips[: c.parts], strips[c.parts :])
         s.western(row)
     top = lambda i: HALO + i - (DEPTH - 1)
     bottom = lambda i: HALO + rows - 1 - i
@@ -352,11 +359,11 @@
     vmem, hbm = pl.BlockSpec(memory_space=pltpu.VMEM), pl.BlockSpec(memory_space=pltpu.HBM)
     params = pltpu.CompilerParams(vmem_limit_bytes=8 * 1024 * 1024)
 
-    fields, one, two, lat_one, lat_two = pl.pallas_call(
+    fields, one, two, early = pl.pallas_call(
         functools.partial(pack_kernel, c),
-        out_shape=(f32(c.count, rows, lanes), *(f32(c.parts, rows, lanes),) * 2, *(f32(c.first, TILE, lanes),) * 2),
+        out_shape=(f32(c.count, rows, lanes), *(f32(c.parts, rows, lanes),) * 2, f32(c.early, TILE, lanes)),
         in_specs=[hbm] * 6,
-        out_specs=(vmem,) * 5,
+        out_specs=(vmem,) * 4,
         scratch_shapes=[
             pltpu.VMEM((levels, rows, lanes), jnp.float32),
             pltpu.VMEM((levels, rows, lanes), jnp.float32),
@@ -372,17 +379,18 @@
     one = lax.ppermute(one, "lon", swaps(lon, 0))
     two = lax.ppermute(two, "lon", swaps(lon, 1))
     both = ("lat", "lon")
-    lat_pairs, other_pairs = lat_swaps(lat, lon, 0), lat_swaps(lat, lon, 1)
-    first = lax.ppermute(lat_one, both, lat_pairs), lax.ppermute(lat_two, both, other_pairs)
-    lat_one, lat_two = pl.pallas_call(
+    early_pairs, late_pairs = lat_swaps(lat, lon, 0), lat_swaps(lat, lon, 1)
+    early = lax.ppermute(early, both, early_pairs)
+    early_strips, late = pl.pallas_call(
         functools.partial(corner_kernel, c),
-        out_shape=(f32(c.second, TILE, lanes),) * 2,
+        out_shape=(f32(c.strips, TILE, lanes), f32(c.late, TILE, lanes)),
         in_specs=[vmem] * 3,
         out_specs=(vmem,) * 2,
         compiler_params=params,
-        name="corners",
-    )(fields, one, two)
-    second = lax.ppermute(lat_one, both, lat_pairs), lax.ppermute(lat_two, both, other_pairs)
+        name="late_rows",
+    )(fields, two, one)
+    late = lax.ppermute(late, both, late_pairs)
+    early_strips = lax.ppermute(early_strips, both, early_pairs)
     twice = lambda *shape: (f32(*shape), f32(*shape))
     shapes = (
         *twice(c.count, span, lanes),
@@ -405,17 +413,17 @@
             flops=2 * STEPS * levels * rows * lanes * 40, bytes_accessed=16 * 2**20, transcendentals=0
         ),
         name="own_rows",
-    )(fields, one, two)
+    )(fields, two, one)
     out = pl.pallas_call(
         functools.partial(edge_kernel, c),
         out_shape=(*shapes, *(f32(levels, rows, lanes),) * 3),
-        in_specs=[vmem] * (4 + len(shapes)),
+        in_specs=[vmem] * (3 + len(shapes)),
         out_specs=(*(vmem,) * len(shapes), hbm, hbm, hbm),
-        input_output_aliases={4 + i: i for i in range(len(shapes))},
+        input_output_aliases={3 + i: i for i in range(len(shapes))},
         scratch_shapes=[pltpu.SemaphoreType.DMA((3,))],
         compiler_params=params,
         name="edge_rows",
-    )(*first, *second[::-1], *own)
+    )(late, early, early_strips, *own)
     return tuple(out[len(shapes) :])
 
 

time: 14.3 us -> 15 us (1.049)
  starting transfers between devices: 7.71 us -> 8.6 us
    ppermute x4 -> x3, starting transfers between devices: 4.58 us -> 5.49 us  [the longest x1 3.65 us: body(): early_strips = lax.ppermute(early_strips, both, early_pairs)]
    ppermute x1, waiting for transfers between devices: 0.49 us -> 0.01 us  [body(): two = lax.ppermute(two, 'lon', swaps(lon, 1))]
    ppermute x4 -> x3, waiting for transfers between devices: 0.01 us -> 0.37 us  [the longest x1 0.36 us: body(): early_strips = lax.ppermute(early_strips, both, early_pairs)]
    ppermute x1, starting transfers between devices: 2.61 us -> 2.44 us  [body(): two = lax.ppermute(two, 'lon', swaps(lon, 1))]
    ppermute x1, starting transfers between devices: 0.52 us -> 0.68 us  [body(): one = lax.ppermute(one, 'lon', swaps(lon, 0))]
  transfers between devices with their start and end apart: 6 -> 5, of which waited for: 1 -> 1; matrix products, arithmetic and copies ran while one was open for 0% -> 0% of each run, Pallas kernels for 14% -> 14%
where the time goes in v1:
time: 15 us; the launch traced here: 14.8 us
  starting transfers between devices  8.6 us (57%)
  Pallas kernels  5.19 us (35%)
  between operations  0.66 us (4%)
  waiting for transfers between devices  0.37 us (2%)
    ppermute x1, starting transfers between devices, body(): early_strips = lax.ppermute(early_strips, both, early_pairs)  3.65 us
    ppermute x1, starting transfers between devices, body(): two = lax.ppermute(two, 'lon', swaps(lon, 1))  2.44 us
    pallas_call x1, Pallas kernels, body(): pl.pallas_call(functools.partial(own_kernel, c), out_shape=shapes, in_spe...  1.99 us
    pallas_call x1, Pallas kernels, body(): pl.pallas_call(functools.partial(edge_kernel, c), out_shape=(*shapes, *(f...  1.73 us
    ppermute x1, starting transfers between devices, body(): early = lax.ppermute(early, both, early_pairs)  1.52 us
    pallas_call x1, Pallas kernels, body(): pl.pallas_call(functools.partial(pack_kernel, c), out_shape=(f32(c.count,...  1.44 us
    ppermute x1, starting transfers between devices, body(): one = lax.ppermute(one, 'lon', swaps(lon, 0))  0.68 us
    ppermute x1, waiting for transfers between devices, body(): early_strips = lax.ppermute(early_strips, both, early_pairs)  0.36 us
  transfers between devices with their start and end apart: 5, of which 1 were waited for; matrix products, arithmetic and copies ran while one was open for 0% of the time, Pallas kernels for 14%

profile of v1, /device:TPU:0, one launch (start us, length us, event | category | flops | bytes accessed | tf_op | source)
XLA Modules:
  0.0 14.8 jit_solution(14442694475588270092)
XLA Ops:
  0.6 1.4 %pack.1 = (f32[26,48,128]{2,1,0:T(8,128)S(1)}, f32[2,48,128]{2,1,0:T(8,128)S(1)}, f32[2,48,128]{2,1,0:T(8,128)S(1)}, f32[28,8,128]{2,1,0:T(8,128)S(1)}) custom-call(f32[6,48,128]{2,1,0:T(8,128)} %u_hbm.1, f32[6,48,128]{2,1,0:T(8,128)} %s_hbm.1, f32[6,48,128]{2,1,0:T(8,128)} %a_hbm.1, f32[2,48,128]{2,1,0:T(8,128)} %c_hbm.1, s32[6,48,128]{2,1,0:T(8,128)} %land_hbm.1, ...), custom_call_target="tpu_custom_call" | custom-call | tf_op jit(solution)/shard_map/pack/pallas_call | solution.py:362
  2.1 2.4 %collective-permute-start = (f32[2,48,128]{2,1,0:T(8,128)S(1)}, f32[2,48,128]{2,1,0:T(8,128)S(1)}, u32[]{:S(2)}, u32[]{:S(2)}) collective-permute-start(f32[2,48,128]{2,1,0:T(8,128)S(1)} %get-tuple-element.27), channel_id=1, source_target_pairs={{1,2},{3,0},{2,1},{0,3},{5,6},{7,4},{6,5},{4,7},{9,10},{11,8},{10,... | collective-permute-start | bytes 147464 | tf_op jit(solution)/shard_map/ppermute | solution.py:380
  4.5 0.7 %collective-permute-start.1 = (f32[2,48,128]{2,1,0:T(8,128)S(1)}, f32[2,48,128]{2,1,0:T(8,128)S(1)}, u32[]{:S(2)}, u32[]{:S(2)}) collective-permute-start(f32[2,48,128]{2,1,0:T(8,128)S(1)} %get-tuple-element.28), channel_id=1, source_target_pairs={{0,1},{2,3},{1,0},{3,2},{4,5},{6,7},{5,4},{7,6},{8,9},{10,11},{9,8... | collective-permute-start | bytes 147464 | tf_op jit(solution)/shard_map/ppermute | solution.py:379
  5.2 1.5 %collective-permute-start.3 = (f32[28,8,128]{2,1,0:T(8,128)S(1)}, f32[28,8,128]{2,1,0:T(8,128)S(1)}, u32[]{:S(2)}, u32[]{:S(2)}) collective-permute-start(f32[28,8,128]{2,1,0:T(8,128)S(1)} %get-tuple-element.30), channel_id=1, source_target_pairs={{0,4},{1,5},{2,6},{3,7},{8,12},{9,13},{10,14},{11,15},{16,20},{17,... | collective-permute-start | bytes 344072 | tf_op jit(solution)/shard_map/ppermute | solution.py:383
  6.7 0.0 collective-permute-done.two_ref
  6.7 0.0 collective-permute-done.1.one_ref
  6.8 0.3 %collective-permute-start.2 = (f32[27,8,128]{2,1,0:T(8,128)S(1)}, f32[27,8,128]{2,1,0:T(8,128)S(1)}, u32[]{:S(2)}, u32[]{:S(2)}) collective-permute-start(f32[27,8,128]{2,1,0:T(8,128)S(1)} %get-tuple-element.29), channel_id=1, source_target_pairs={{4,8},{5,9},{6,10},{7,11},{12,16},{13,17},{14,18},{15,19},{20,24},... | collective-permute-start | bytes 331784 | tf_op jit(solution)/shard_map/ppermute | solution.py:392
  7.1 3.6 %collective-permute-start.4 = (f32[4,8,128]{2,1,0:T(8,128)S(1)}, f32[4,8,128]{2,1,0:T(8,128)S(1)}, u32[]{:S(2)}, u32[]{:S(2)}) collective-permute-start(f32[4,8,128]{2,1,0:T(8,128)S(1)} %get-tuple-element.31), channel_id=1, source_target_pairs={{0,4},{1,5},{2,6},{3,7},{8,12},{9,13},{10,14},{11,15},{16,20},{17,... | collective-permute-start | bytes 49160 | tf_op jit(solution)/shard_map/ppermute | solution.py:393
  10.7 2.0 %own_rows.1 = (f32[26,64,128]{2,1,0:T(8,128)S(1)}, f32[26,64,128]{2,1,0:T(8,128)S(1)}, f32[64,128]{1,0:T(8,128)S(1)}, f32[64,128]{1,0:T(8,128)S(1)}, f32[6,64,12...) custom-call(f32[26,48,128]{2,1,0:T(8,128)S(1)} %get-tuple-element.26, ...), custom_call_target="tpu_custom_call" | custom-call | flops 11796480 | bytes 16777216 | tf_op jit(solution)/shard_map/own_rows/pallas_call | solution.py:406
  12.7 0.4 %collective-permute-done.4.early_strips = f32[4,8,128]{2,1,0:T(8,128)S(1)} collective-permute-done((f32[4,8,128]{2,1,0:T(8,128)S(1)}, f32[4,8,128]{2,1,0:T(8,128)S(1)}, u32[]{:S(2)}, u32[]{:S(2)}) %collective-permute-start.4) | collective-permute-done | bytes 16416 | tf_op jit(solution)/shard_map/ppermute | solution.py:393
  13.1 0.0 collective-permute-done.3.early
  13.1 0.0 collective-permute-done.2.late
  13.1 1.7 %edge_rows.1 = (f32[26,64,128]{2,1,0:T(8,128)S(1)}, f32[26,64,128]{2,1,0:T(8,128)S(1)}, f32[64,128]{1,0:T(8,128)S(1)}, f32[64,128]{1,0:T(8,128)S(1)}, f32[6,64,1...) custom-call(f32[27,8,128]{2,1,0:T(8,128)S(1)} %collective-permute-do, ...), custom_call_target="tpu_custom_call", output_to_operand_aliasing={{0}: (3, {}), {1}: (4, {}), {2}: (5, {}), {3}: (6, {}), {4}... | custom-call | tf_op jit(solution)/shard_map/edge_rows/pallas_call | solution.py:417
  (1 shorter events, 0.0 us)
Async XLA Ops:
  2.1 4.6 %collective-permute-start = (f32[2,48,128]{2,1,0:T(8,128)S(1)}, f32[2,48,128]{2,1,0:T(8,128)S(1)}, u32[]{:S(2)}, u32[]{:S(2)}) collective-permute-start(f32[2,48,128]{2,1,0:T(8,128)S(1)} %get-tuple-element.27), channel_id=1, source_target_pairs={{1,2},{3,0},{2,1},{0,3},{5,6},{7,4},{6,5},{4,7},{9,10},{11,8},{10,... | collective-permute-start | bytes 147464 | tf_op jit(solution)/shard_map/ppermute | solution.py:380
  4.5 2.2 %collective-permute-start.1 = (f32[2,48,128]{2,1,0:T(8,128)S(1)}, f32[2,48,128]{2,1,0:T(8,128)S(1)}, u32[]{:S(2)}, u32[]{:S(2)}) collective-permute-start(f32[2,48,128]{2,1,0:T(8,128)S(1)} %get-tuple-element.28), channel_id=1, source_target_pairs={{0,1},{2,3},{1,0},{3,2},{4,5},{6,7},{5,4},{7,6},{8,9},{10,11},{9,8... | collective-permute-start | bytes 147464 | tf_op jit(solution)/shard_map/ppermute | solution.py:379
  5.2 7.9 %collective-permute-start.3 = (f32[28,8,128]{2,1,0:T(8,128)S(1)}, f32[28,8,128]{2,1,0:T(8,128)S(1)}, u32[]{:S(2)}, u32[]{:S(2)}) collective-permute-start(f32[28,8,128]{2,1,0:T(8,128)S(1)} %get-tuple-element.30), channel_id=1, source_target_pairs={{0,4},{1,5},{2,6},{3,7},{8,12},{9,13},{10,14},{11,15},{16,20},{17,... | collective-permute-start | bytes 344072 | tf_op jit(solution)/shard_map/ppermute | solution.py:383
  6.8 6.3 %collective-permute-start.2 = (f32[27,8,128]{2,1,0:T(8,128)S(1)}, f32[27,8,128]{2,1,0:T(8,128)S(1)}, u32[]{:S(2)}, u32[]{:S(2)}) collective-permute-start(f32[27,8,128]{2,1,0:T(8,128)S(1)} %get-tuple-element.29), channel_id=1, source_target_pairs={{4,8},{5,9},{6,10},{7,11},{12,16},{13,17},{14,18},{15,19},{20,24},... | collective-permute-start | bytes 331784 | tf_op jit(solution)/shard_map/ppermute | solution.py:392
  7.1 6.0 %collective-permute-start.4 = (f32[4,8,128]{2,1,0:T(8,128)S(1)}, f32[4,8,128]{2,1,0:T(8,128)S(1)}, u32[]{:S(2)}, u32[]{:S(2)}) collective-permute-start(f32[4,8,128]{2,1,0:T(8,128)S(1)} %get-tuple-element.31), channel_id=1, source_target_pairs={{0,4},{1,5},{2,6},{3,7},{8,12},{9,13},{10,14},{11,15},{16,20},{17,... | collective-permute-start | bytes 49160 | tf_op jit(solution)/shard_map/ppermute | solution.py:393

commit v2 on v0

--- a/solution.py
+++ b/solution.py
@@ -11,6 +11,7 @@
 DEPTH = 2 * STEPS
 TILE = 8
 HALO = TILE
+PIECE = 2
 
 vertical_coef = 0.04
 
@@ -55,29 +56,29 @@
 ):
     levels = c.levels
     _, rows, lanes = u_ref.shape
-    moves = [
-        pltpu.make_async_copy(source, target, sems.at[i])
-        for i, (source, target) in enumerate(
-            (
-                (bottom_hbm, bottom_ref),
-                (land_hbm, land_ref),
-                (u_hbm, u_ref),
-                (s_hbm, s_ref),
-                (c_hbm, c_ref),
-                (a_hbm, f_ref.at[pl.ds(c.cot, levels)]),
-            )
-        )
-    ]
+    pieces = [(bottom_hbm, bottom_ref)]
+    groups = [range(k, min(k + PIECE, levels)) for k in range(0, levels, PIECE)]
+    for held in groups:
+        at = pl.ds(held.start, len(held))
+        pieces += [(land_hbm.at[at], land_ref.at[at]), (u_hbm.at[at], u_ref.at[at]), (s_hbm.at[at], s_ref.at[at])]
+    pieces.append((c_hbm, c_ref))
+    for held in groups:
+        pieces.append((a_hbm.at[pl.ds(held.start, len(held))], f_ref.at[pl.ds(c.cot + held.start, len(held))]))
+    moves = [pltpu.make_async_copy(source, target, sems.at[i]) for i, (source, target) in enumerate(pieces)]
     for move in moves:
         move.start()
-    for move in moves:
+    last_lat = lax.axis_index("lat") == lax.axis_size("lat") - 1
+    moves[0].wait()
+    for i, held in enumerate(groups):
+        for move in moves[1 + 3 * i : 4 + 3 * i]:
+            move.wait()
+        for k in held:
+            wet = jnp.where(k < bottom_ref[...], land_ref[k], 0).astype(jnp.float32)
+            f_ref[c.u + k] = wet * u_ref[k]
+            f_ref[c.s + k] = wet * s_ref[k]
+            f_ref[c.wet + k] = wet
+    for move in moves[1 + 3 * len(groups) :]:
         move.wait()
-    last_lat = lax.axis_index("lat") == lax.axis_size("lat") - 1
-    for k in range(levels):
-        wet = jnp.where(k < bottom_ref[...], land_ref[k], 0).astype(jnp.float32)
-        f_ref[c.u + k] = wet * u_ref[k]
-        f_ref[c.s + k] = wet * s_ref[k]
-        f_ref[c.wet + k] = wet
     f_ref[c.ce] = c_ref[0]
     row = lax.broadcasted_iota(jnp.int32, (rows, lanes), 0)
     f_ref[c.cn] = jnp.where(jnp.logical_and(last_lat, row == rows - 1), 0.0, c_ref[1])
@@ -278,6 +279,23 @@
     e0, e1, w0, w1, d0, d1, x0, x1, m0, m1, adj, state, grad, gsource, state_hbm, grad_hbm, gsource_hbm, sems = refs[14:]
     rows = grad.shape[1]
     s = Sweeps(c, (e0, e1), (w0, w1), (d0, d1), (x0, x1), (m0, m1), adj, state)
+    moves = []
+
+    def send(ref, skip, target, at, many):
+        move = pltpu.make_async_copy(
+            ref.at[:, pl.ds(skip + at, many), :], target.at[:, pl.ds(at, many), :], sems.at[len(moves)]
+        )
+        move.start()
+        moves.append(move)
+
+    def send_edges(ref, skip, target):
+        send(ref, skip, target, 0, TILE)
+        send(ref, skip, target, rows - TILE, TILE)
+
+    inner = rows - 2 * TILE
+    send(state, HALO, state_hbm, TILE, inner)
+    send(gsource, 0, gsource_hbm, TILE, inner)
+    send(grad, 0, grad_hbm, TILE, inner)
     odd_lat = is_odd("lat")
     for row, low in ((0, True), (HALO + rows, False)):
         pole = lax.axis_index("lat") == (0 if low else lax.axis_size("lat") - 1)
@@ -306,24 +324,18 @@
     for n in range(STEPS):
         for row in places(n):
             s.forward(n, row)
-    own = pl.ds(HALO, rows)
-    moves = [
-        pltpu.make_async_copy(state.at[:, own, :], state_hbm, sems.at[0]),
-        pltpu.make_async_copy(gsource, gsource_hbm, sems.at[1]),
-        pltpu.make_async_copy(grad, grad_hbm, sems.at[2]),
-    ]
-    moves[0].start()
+    send_edges(state, HALO, state_hbm)
     for n in range(STEPS - 1, 0, -1):
         for row in places(2 * STEPS - 1 - n):
             s.backward(n, row)
     for row in places(DEPTH - 1):
         for k, value in s.source_gradient(row):
             gsource[k, pl.ds(row - HALO, TILE), :] = value
-    moves[1].start()
+    send_edges(gsource, 0, gsource_hbm)
     for row in places(DEPTH - 1):
         for k, value in s.gradient(row):
             grad[k, pl.ds(row - HALO, TILE), :] = value
-    moves[2].start()
+    send_edges(grad, 0, grad_hbm)
     for move in moves:
         move.wait()
 
@@ -363,7 +375,7 @@
             pltpu.VMEM((2, rows, lanes), jnp.float32),
             pltpu.VMEM((levels, rows, lanes), jnp.int32),
             pltpu.VMEM((rows, lanes), jnp.int32),
-            pltpu.SemaphoreType.DMA((6,)),
+            pltpu.SemaphoreType.DMA((2 + 4 * -(-levels // PIECE),)),
         ],
         compiler_params=params,
         name="pack",
@@ -412,7 +424,7 @@
         in_specs=[vmem] * (4 + len(shapes)),
         out_specs=(*(vmem,) * len(shapes), hbm, hbm, hbm),
         input_output_aliases={4 + i: i for i in range(len(shapes))},
-        scratch_shapes=[pltpu.SemaphoreType.DMA((3,))],
+        scratch_shapes=[pltpu.SemaphoreType.DMA((9,))],
         compiler_params=params,
         name="edge_rows",
     )(*first, *second[::-1], *own)

time: 14.3 us -> 14.3 us (level)
  no operation moved by 1% of the time
where the time goes in v2:
time: 14.3 us; the launch traced here: 14.1 us
  starting transfers between devices  7.71 us (54%)
  Pallas kernels  5.22 us (37%)
  between operations  0.68 us (5%)
  waiting for transfers between devices  0.51 us (4%)
    ppermute x2, starting transfers between devices, body(): lax.ppermute(lat_one, both, lat_pairs)  4.4 us
    ppermute x1, starting transfers between devices, body(): two = lax.ppermute(two, 'lon', swaps(lon, 1))  2.61 us
    pallas_call x1, Pallas kernels, body(): pl.pallas_call(functools.partial(own_kernel, c), out_shape=shapes, in_spe...  2.03 us
    pallas_call x1, Pallas kernels, body(): pl.pallas_call(functools.partial(edge_kernel, c), out_shape=(*shapes, *(f...  1.74 us
    pallas_call x1, Pallas kernels, body(): pl.pallas_call(functools.partial(pack_kernel, c), out_shape=(f32(c.count,...  1.43 us
    ppermute x1, starting transfers between devices, body(): one = lax.ppermute(one, 'lon', swaps(lon, 0))  0.52 us
    ppermute x1, waiting for transfers between devices, body(): two = lax.ppermute(two, 'lon', swaps(lon, 1))  0.49 us
  transfers between devices with their start and end apart: 6, of which 1 were waited for; matrix products, arithmetic and copies ran while one was open for 0% of the time, Pallas kernels for 14%

profile of v2, /device:TPU:0, one launch (start us, length us, event | category | flops | bytes accessed | tf_op | source)
XLA Modules:
  0.0 14.1 jit_solution(6625682699963281544)
XLA Ops:
  0.6 1.4 %pack.1 = (f32[26,48,128]{2,1,0:T(8,128)S(1)}, f32[2,48,128]{2,1,0:T(8,128)S(1)}, f32[2,48,128]{2,1,0:T(8,128)S(1)}, f32[18,8,128]{2,1,0:T(8,128)S(1)}, f32[18,8,128]{2,1,0:T(8,128)S(1)}) custom-call(f32[6,48,128]{2,1,0:T(8,128)} %u_hbm.1, f32[6,48,128]{2,1,0:T(8,128)} %s_hbm.1, f32[6,48,128]{2,1,0:T(8,128)} %a_hbm.1, f32[2,48,128]{2,1,0:T(8,128)} %c_hbm.1, ...), custom_call_target="tpu_custom_call" | custom-call | tf_op jit(solution)/shard_map/pack/pallas_call | solution.py:367
  2.1 0.5 %collective-permute-start.2 = (f32[2,48,128]{2,1,0:T(8,128)S(1)}, f32[2,48,128]{2,1,0:T(8,128)S(1)}, u32[]{:S(2)}, u32[]{:S(2)}) collective-permute-start(f32[2,48,128]{2,1,0:T(8,128)S(1)} %get-tuple-element.30), channel_id=1, source_target_pairs={{0,1},{2,3},{1,0},{3,2},{4,5},{6,7},{5,4},{7,6},{8,9},{10,11},{9,8... | collective-permute-start | bytes 147464 | tf_op jit(solution)/shard_map/ppermute | solution.py:384
  2.6 2.6 %collective-permute-start.3 = (f32[2,48,128]{2,1,0:T(8,128)S(1)}, f32[2,48,128]{2,1,0:T(8,128)S(1)}, u32[]{:S(2)}, u32[]{:S(2)}) collective-permute-start(f32[2,48,128]{2,1,0:T(8,128)S(1)} %get-tuple-element.31), channel_id=1, source_target_pairs={{1,2},{3,0},{2,1},{0,3},{5,6},{7,4},{6,5},{4,7},{9,10},{11,8},{10,... | collective-permute-start | bytes 147464 | tf_op jit(solution)/shard_map/ppermute | solution.py:385
  5.2 1.5 %collective-permute-start = (f32[18,8,128]{2,1,0:T(8,128)S(1)}, f32[18,8,128]{2,1,0:T(8,128)S(1)}, u32[]{:S(2)}, u32[]{:S(2)}) collective-permute-start(f32[18,8,128]{2,1,0:T(8,128)S(1)} %get-tuple-element.27), channel_id=1, source_target_pairs={{0,4},{1,5},{2,6},{3,7},{8,12},{9,13},{10,14},{11,15},{16,20},{17,... | collective-permute-start | bytes 221192 | tf_op jit(solution)/shard_map/ppermute | solution.py:388
  6.7 0.0 collective-permute-start.1
  6.7 0.0 collective-permute-done.2.one_ref
  6.7 0.5 %collective-permute-done.3.two_ref = f32[2,48,128]{2,1,0:T(8,128)S(1)} collective-permute-done((f32[2,48,128]{2,1,0:T(8,128)S(1)}, f32[2,48,128]{2,1,0:T(8,128)S(1)}, u32[]{:S(2)}, u32[]{:S(2)}) %collective-permute-start.3) | collective-permute-done | bytes 49184 | tf_op jit(solution)/shard_map/ppermute | solution.py:385
  7.2 0.2 %collective-permute-start.4 = (f32[9,8,128]{2,1,0:T(8,128)S(1)}, f32[9,8,128]{2,1,0:T(8,128)S(1)}, u32[]{:S(2)}, u32[]{:S(2)}) collective-permute-start(f32[9,8,128]{2,1,0:T(8,128)S(1)} %get-tuple-element.32), channel_id=1, source_target_pairs={{4,8},{5,9},{6,10},{7,11},{12,16},{13,17},{14,18},{15,19},{20,24},... | collective-permute-start | bytes 110600 | tf_op jit(solution)/shard_map/ppermute | solution.py:397
  7.4 2.9 %collective-permute-start.5 = (f32[9,8,128]{2,1,0:T(8,128)S(1)}, f32[9,8,128]{2,1,0:T(8,128)S(1)}, u32[]{:S(2)}, u32[]{:S(2)}) collective-permute-start(f32[9,8,128]{2,1,0:T(8,128)S(1)} %get-tuple-element.33), channel_id=1, source_target_pairs={{0,4},{1,5},{2,6},{3,7},{8,12},{9,13},{10,14},{11,15},{16,20},{17,... | collective-permute-start | bytes 110600 | tf_op jit(solution)/shard_map/ppermute | solution.py:397
  10.3 2.0 %own_rows.1 = (f32[26,64,128]{2,1,0:T(8,128)S(1)}, f32[26,64,128]{2,1,0:T(8,128)S(1)}, f32[64,128]{1,0:T(8,128)S(1)}, f32[64,128]{1,0:T(8,128)S(1)}, f32[6,64,12...) custom-call(f32[26,48,128]{2,1,0:T(8,128)S(1)} %get-tuple-element.29, ...), custom_call_target="tpu_custom_call" | custom-call | flops 11796480 | bytes 16777216 | tf_op jit(solution)/shard_map/own_rows/pallas_call | solution.py:410
  12.3 0.0 collective-permute-done.first_one
  12.3 0.0 collective-permute-done.1.first_two
  12.4 0.0 collective-permute-done.4.second_two
  12.4 0.0 collective-permute-done.5.second_one
  12.4 1.7 %edge_rows.1 = (f32[26,64,128]{2,1,0:T(8,128)S(1)}, f32[26,64,128]{2,1,0:T(8,128)S(1)}, f32[64,128]{1,0:T(8,128)S(1)}, f32[64,128]{1,0:T(8,128)S(1)}, f32[6,64,1...) custom-call(f32[18,8,128]{2,1,0:T(8,128)S(1)} %collective-permute-do, ...), custom_call_target="tpu_custom_call", output_to_operand_aliasing={{0}: (4, {}), {1}: (5, {}), {2}: (6, {}), {3}: (7, {}), {4}... | custom-call | tf_op jit(solution)/shard_map/edge_rows/pallas_call | solution.py:421
  (1 shorter events, 0.0 us)
Async XLA Ops:
  2.1 4.7 %collective-permute-start.2 = (f32[2,48,128]{2,1,0:T(8,128)S(1)}, f32[2,48,128]{2,1,0:T(8,128)S(1)}, u32[]{:S(2)}, u32[]{:S(2)}) collective-permute-start(f32[2,48,128]{2,1,0:T(8,128)S(1)} %get-tuple-element.30), channel_id=1, source_target_pairs={{0,1},{2,3},{1,0},{3,2},{4,5},{6,7},{5,4},{7,6},{8,9},{10,11},{9,8... | collective-permute-start | bytes 147464 | tf_op jit(solution)/shard_map/ppermute | solution.py:384
  2.6 4.6 %collective-permute-start.3 = (f32[2,48,128]{2,1,0:T(8,128)S(1)}, f32[2,48,128]{2,1,0:T(8,128)S(1)}, u32[]{:S(2)}, u32[]{:S(2)}) collective-permute-start(f32[2,48,128]{2,1,0:T(8,128)S(1)} %get-tuple-element.31), channel_id=1, source_target_pairs={{1,2},{3,0},{2,1},{0,3},{5,6},{7,4},{6,5},{4,7},{9,10},{11,8},{10,... | collective-permute-start | bytes 147464 | tf_op jit(solution)/shard_map/ppermute | solution.py:385
  5.2 7.1 %collective-permute-start = (f32[18,8,128]{2,1,0:T(8,128)S(1)}, f32[18,8,128]{2,1,0:T(8,128)S(1)}, u32[]{:S(2)}, u32[]{:S(2)}) collective-permute-start(f32[18,8,128]{2,1,0:T(8,128)S(1)} %get-tuple-element.27), channel_id=1, source_target_pairs={{0,4},{1,5},{2,6},{3,7},{8,12},{9,13},{10,14},{11,15},{16,20},{17,... | collective-permute-start | bytes 221192 | tf_op jit(solution)/shard_map/ppermute | solution.py:388
  6.7 5.6 %collective-permute-start.1 = (f32[18,8,128]{2,1,0:T(8,128)S(1)}, f32[18,8,128]{2,1,0:T(8,128)S(1)}, u32[]{:S(2)}, u32[]{:S(2)}) collective-permute-start(f32[18,8,128]{2,1,0:T(8,128)S(1)} %get-tuple-element.28), channel_id=1, source_target_pairs={{4,8},{5,9},{6,10},{7,11},{12,16},{13,17},{14,18},{15,19},{20,24},... | collective-permute-start | bytes 221192 | tf_op jit(solution)/shard_map/ppermute | solution.py:388
  7.2 5.1 %collective-permute-start.4 = (f32[9,8,128]{2,1,0:T(8,128)S(1)}, f32[9,8,128]{2,1,0:T(8,128)S(1)}, u32[]{:S(2)}, u32[]{:S(2)}) collective-permute-start(f32[9,8,128]{2,1,0:T(8,128)S(1)} %get-tuple-element.32), channel_id=1, source_target_pairs={{4,8},{5,9},{6,10},{7,11},{12,16},{13,17},{14,18},{15,19},{20,24},... | collective-permute-start | bytes 110600 | tf_op jit(solution)/shard_map/ppermute | solution.py:397
  7.4 4.9 %collective-permute-start.5 = (f32[9,8,128]{2,1,0:T(8,128)S(1)}, f32[9,8,128]{2,1,0:T(8,128)S(1)}, u32[]{:S(2)}, u32[]{:S(2)}) collective-permute-start(f32[9,8,128]{2,1,0:T(8,128)S(1)} %get-tuple-element.33), channel_id=1, source_target_pairs={{0,4},{1,5},{2,6},{3,7},{8,12},{9,13},{10,14},{11,15},{16,20},{17,... | collective-permute-start | bytes 110600 | tf_op jit(solution)/shard_map/ppermute | solution.py:397

commit v3 on v2

--- a/solution.py
+++ b/solution.py
@@ -134,6 +134,7 @@
 class Sweeps:
     def __init__(self, c, e, w, d, x, m, adj, state):
         self.c, self.e, self.w, self.d, self.x, self.m, self.adj, self.state = c, e, w, d, x, m, adj, state
+        self.held = []
         self.lanes = e[0].shape[-1]
         lane = lane_iota(self.lanes)
         self.at_first, self.at_last = lane == 0, lane == self.lanes - 1
@@ -180,11 +181,19 @@
             out.append(pair)
         return out
 
+    def put(self, ref, k, at, value):
+        self.held.append((ref, k, at, value))
+
+    def flush(self):
+        for ref, k, at, value in self.held:
+            ref[k, at, :] = value
+        self.held = []
+
     def diagonal(self, row):
         load = lambda h, k, at: self.e[h][self.c.wet + k, at, :]
         for k, pair in enumerate(self.neighbours(load, row)):
             for h, (_, total) in enumerate(pair):
-                self.d[h][k, pl.ds(row, TILE), :] = 1.0 - total
+                self.put(self.d[h], k, pl.ds(row, TILE), 1.0 - total)
 
     def loader(self, index):
         if index == 0:
@@ -201,12 +210,12 @@
                 bounded = wet * jnp.tanh(self.d[h][k, at, :] * own + total)
                 slope = wet - bounded * bounded
                 if n < STEPS - 1:
-                    self.x[h][n * c.levels + k, at, :] = bounded + e[c.s + k, at, :]
-                    self.m[h][n * c.levels + k, at, :] = slope
+                    self.put(self.x[h], n * c.levels + k, at, bounded + e[c.s + k, at, :])
+                    self.put(self.m[h], n * c.levels + k, at, slope)
                 else:
                     if h == 0:
-                        self.state[k, at, :] = bounded + e[c.s + k, at, :]
-                    self.x[h][n * c.levels + k, at, :] = slope * e[c.cot + k, at, :]
+                        self.put(self.state, k, at, bounded + e[c.s + k, at, :])
+                    self.put(self.x[h], n * c.levels + k, at, slope * e[c.cot + k, at, :])
 
     def backward(self, n, row):
         c, at = self.c, pl.ds(row, TILE)
@@ -215,8 +224,15 @@
             for h, (own, total) in enumerate(pair):
                 value = self.d[h][k, at, :] * own + total
                 if h == 0:
-                    self.adj[(n - 1) * c.levels + k, at, :] = value
-                self.x[h][index * c.levels + k, at, :] = self.m[h][(n - 1) * c.levels + k, at, :] * value
+                    self.put(self.adj, (n - 1) * c.levels + k, at, value)
+                self.put(self.x[h], index * c.levels + k, at, self.m[h][(n - 1) * c.levels + k, at, :] * value)
+
+    def over(self, step, rows, together):
+        for i, row in enumerate(rows):
+            step(row)
+            if (i + 1) % together == 0:
+                self.flush()
+        self.flush()
 
     def gradient(self, row):
         c, at = self.c, pl.ds(row, TILE)
@@ -255,14 +271,11 @@
             [jnp.where(odd_lon, one, two) for one, two in pairs],
         )
         s.western(row)
-    for row in places:
-        s.diagonal(row)
+    s.over(s.diagonal, places, 1)
     for n in range(STEPS):
-        for row in places:
-            s.forward(n, row)
+        s.over(functools.partial(s.forward, n), places, 1)
     for n in range(STEPS - 1, 0, -1):
-        for row in places:
-            s.backward(n, row)
+        s.over(functools.partial(s.backward, n), places, 1)
     for row in places[1:-1]:
         at = pl.ds(row - HALO, TILE)
         for k, value in s.source_gradient(row):
@@ -319,22 +332,21 @@
     top = lambda i: HALO + i - (DEPTH - 1)
     bottom = lambda i: HALO + rows - 1 - i
     places = lambda i: (top(i), bottom(i))
-    for row in places(0):
-        s.diagonal(row)
+    s.over(s.diagonal, places(0), 2)
     for n in range(STEPS):
-        for row in places(n):
-            s.forward(n, row)
+        s.over(functools.partial(s.forward, n), places(n), 2)
     send_edges(state, HALO, state_hbm)
     for n in range(STEPS - 1, 0, -1):
-        for row in places(2 * STEPS - 1 - n):
-            s.backward(n, row)
+        s.over(functools.partial(s.backward, n), places(2 * STEPS - 1 - n), 2)
     for row in places(DEPTH - 1):
         for k, value in s.source_gradient(row):
-            gsource[k, pl.ds(row - HALO, TILE), :] = value
+            s.put(gsource, k, pl.ds(row - HALO, TILE), value)
+    s.flush()
     send_edges(gsource, 0, gsource_hbm)
     for row in places(DEPTH - 1):
         for k, value in s.gradient(row):
-            grad[k, pl.ds(row - HALO, TILE), :] = value
+            s.put(grad, k, pl.ds(row - HALO, TILE), value)
+    s.flush()
     send_edges(grad, 0, grad_hbm)
     for move in moves:
         move.wait()

time: 14.3 us -> 14.3 us (level)
  no operation moved by 1% of the time
where the time goes in v3:
time: 14.3 us; the launch traced here: 14.1 us
  starting transfers between devices  7.71 us (54%)
  Pallas kernels  5.21 us (36%)
  between operations  0.68 us (5%)
  waiting for transfers between devices  0.51 us (4%)
    ppermute x2, starting transfers between devices, body(): lax.ppermute(lat_one, both, lat_pairs)  4.4 us
    ppermute x1, starting transfers between devices, body(): two = lax.ppermute(two, 'lon', swaps(lon, 1))  2.61 us
    pallas_call x1, Pallas kernels, body(): pl.pallas_call(functools.partial(own_kernel, c), out_shape=shapes, in_spe...  2.02 us
    pallas_call x1, Pallas kernels, body(): pl.pallas_call(functools.partial(edge_kernel, c), out_shape=(*shapes, *(f...  1.74 us
    pallas_call x1, Pallas kernels, body(): pl.pallas_call(functools.partial(pack_kernel, c), out_shape=(f32(c.count,...  1.43 us
    ppermute x1, starting transfers between devices, body(): one = lax.ppermute(one, 'lon', swaps(lon, 0))  0.52 us
    ppermute x1, waiting for transfers between devices, body(): two = lax.ppermute(two, 'lon', swaps(lon, 1))  0.49 us
  transfers between devices with their start and end apart: 6, of which 1 were waited for; matrix products, arithmetic and copies ran while one was open for 0% of the time, Pallas kernels for 14%

profile of v3, /device:TPU:0, one launch (start us, length us, event | category | flops | bytes accessed | tf_op | source)
XLA Modules:
  0.0 14.1 jit_solution(480116534959733289)
XLA Ops:
  0.6 1.4 %pack.1 = (f32[26,48,128]{2,1,0:T(8,128)S(1)}, f32[2,48,128]{2,1,0:T(8,128)S(1)}, f32[2,48,128]{2,1,0:T(8,128)S(1)}, f32[18,8,128]{2,1,0:T(8,128)S(1)}, f32[18,8,128]{2,1,0:T(8,128)S(1)}) custom-call(f32[6,48,128]{2,1,0:T(8,128)} %u_hbm.1, f32[6,48,128]{2,1,0:T(8,128)} %s_hbm.1, f32[6,48,128]{2,1,0:T(8,128)} %a_hbm.1, f32[2,48,128]{2,1,0:T(8,128)} %c_hbm.1, ...), custom_call_target="tpu_custom_call" | custom-call | tf_op jit(solution)/shard_map/pack/pallas_call | solution.py:379
  2.1 0.5 %collective-permute-start.2 = (f32[2,48,128]{2,1,0:T(8,128)S(1)}, f32[2,48,128]{2,1,0:T(8,128)S(1)}, u32[]{:S(2)}, u32[]{:S(2)}) collective-permute-start(f32[2,48,128]{2,1,0:T(8,128)S(1)} %get-tuple-element.30), channel_id=1, source_target_pairs={{0,1},{2,3},{1,0},{3,2},{4,5},{6,7},{5,4},{7,6},{8,9},{10,11},{9,8... | collective-permute-start | bytes 147464 | tf_op jit(solution)/shard_map/ppermute | solution.py:396
  2.6 2.6 %collective-permute-start.3 = (f32[2,48,128]{2,1,0:T(8,128)S(1)}, f32[2,48,128]{2,1,0:T(8,128)S(1)}, u32[]{:S(2)}, u32[]{:S(2)}) collective-permute-start(f32[2,48,128]{2,1,0:T(8,128)S(1)} %get-tuple-element.31), channel_id=1, source_target_pairs={{1,2},{3,0},{2,1},{0,3},{5,6},{7,4},{6,5},{4,7},{9,10},{11,8},{10,... | collective-permute-start | bytes 147464 | tf_op jit(solution)/shard_map/ppermute | solution.py:397
  5.2 1.5 %collective-permute-start = (f32[18,8,128]{2,1,0:T(8,128)S(1)}, f32[18,8,128]{2,1,0:T(8,128)S(1)}, u32[]{:S(2)}, u32[]{:S(2)}) collective-permute-start(f32[18,8,128]{2,1,0:T(8,128)S(1)} %get-tuple-element.27), channel_id=1, source_target_pairs={{0,4},{1,5},{2,6},{3,7},{8,12},{9,13},{10,14},{11,15},{16,20},{17,... | collective-permute-start | bytes 221192 | tf_op jit(solution)/shard_map/ppermute | solution.py:400
  6.7 0.0 collective-permute-start.1
  6.7 0.0 collective-permute-done.2.one_ref
  6.7 0.5 %collective-permute-done.3.two_ref = f32[2,48,128]{2,1,0:T(8,128)S(1)} collective-permute-done((f32[2,48,128]{2,1,0:T(8,128)S(1)}, f32[2,48,128]{2,1,0:T(8,128)S(1)}, u32[]{:S(2)}, u32[]{:S(2)}) %collective-permute-start.3) | collective-permute-done | bytes 49184 | tf_op jit(solution)/shard_map/ppermute | solution.py:397
  7.2 0.2 %collective-permute-start.4 = (f32[9,8,128]{2,1,0:T(8,128)S(1)}, f32[9,8,128]{2,1,0:T(8,128)S(1)}, u32[]{:S(2)}, u32[]{:S(2)}) collective-permute-start(f32[9,8,128]{2,1,0:T(8,128)S(1)} %get-tuple-element.32), channel_id=1, source_target_pairs={{4,8},{5,9},{6,10},{7,11},{12,16},{13,17},{14,18},{15,19},{20,24},... | collective-permute-start | bytes 110600 | tf_op jit(solution)/shard_map/ppermute | solution.py:409
  7.4 2.9 %collective-permute-start.5 = (f32[9,8,128]{2,1,0:T(8,128)S(1)}, f32[9,8,128]{2,1,0:T(8,128)S(1)}, u32[]{:S(2)}, u32[]{:S(2)}) collective-permute-start(f32[9,8,128]{2,1,0:T(8,128)S(1)} %get-tuple-element.33), channel_id=1, source_target_pairs={{0,4},{1,5},{2,6},{3,7},{8,12},{9,13},{10,14},{11,15},{16,20},{17,... | collective-permute-start | bytes 110600 | tf_op jit(solution)/shard_map/ppermute | solution.py:409
  10.3 2.0 %own_rows.1 = (f32[26,64,128]{2,1,0:T(8,128)S(1)}, f32[26,64,128]{2,1,0:T(8,128)S(1)}, f32[64,128]{1,0:T(8,128)S(1)}, f32[64,128]{1,0:T(8,128)S(1)}, f32[6,64,12...) custom-call(f32[26,48,128]{2,1,0:T(8,128)S(1)} %get-tuple-element.29, ...), custom_call_target="tpu_custom_call" | custom-call | flops 11796480 | bytes 16777216 | tf_op jit(solution)/shard_map/own_rows/pallas_call | solution.py:422
  12.3 0.0 collective-permute-done.first_one
  12.3 0.0 collective-permute-done.1.first_two
  12.3 0.0 collective-permute-done.4.second_two
  12.4 0.0 collective-permute-done.5.second_one
  12.4 1.7 %edge_rows.1 = (f32[26,64,128]{2,1,0:T(8,128)S(1)}, f32[26,64,128]{2,1,0:T(8,128)S(1)}, f32[64,128]{1,0:T(8,128)S(1)}, f32[64,128]{1,0:T(8,128)S(1)}, f32[6,64,1...) custom-call(f32[18,8,128]{2,1,0:T(8,128)S(1)} %collective-permute-do, ...), custom_call_target="tpu_custom_call", output_to_operand_aliasing={{0}: (4, {}), {1}: (5, {}), {2}: (6, {}), {3}: (7, {}), {4}... | custom-call | tf_op jit(solution)/shard_map/edge_rows/pallas_call | solution.py:433
  (1 shorter events, 0.0 us)
Async XLA Ops:
  2.1 4.7 %collective-permute-start.2 = (f32[2,48,128]{2,1,0:T(8,128)S(1)}, f32[2,48,128]{2,1,0:T(8,128)S(1)}, u32[]{:S(2)}, u32[]{:S(2)}) collective-permute-start(f32[2,48,128]{2,1,0:T(8,128)S(1)} %get-tuple-element.30), channel_id=1, source_target_pairs={{0,1},{2,3},{1,0},{3,2},{4,5},{6,7},{5,4},{7,6},{8,9},{10,11},{9,8... | collective-permute-start | bytes 147464 | tf_op jit(solution)/shard_map/ppermute | solution.py:396
  2.6 4.6 %collective-permute-start.3 = (f32[2,48,128]{2,1,0:T(8,128)S(1)}, f32[2,48,128]{2,1,0:T(8,128)S(1)}, u32[]{:S(2)}, u32[]{:S(2)}) collective-permute-start(f32[2,48,128]{2,1,0:T(8,128)S(1)} %get-tuple-element.31), channel_id=1, source_target_pairs={{1,2},{3,0},{2,1},{0,3},{5,6},{7,4},{6,5},{4,7},{9,10},{11,8},{10,... | collective-permute-start | bytes 147464 | tf_op jit(solution)/shard_map/ppermute | solution.py:397
  5.2 7.1 %collective-permute-start = (f32[18,8,128]{2,1,0:T(8,128)S(1)}, f32[18,8,128]{2,1,0:T(8,128)S(1)}, u32[]{:S(2)}, u32[]{:S(2)}) collective-permute-start(f32[18,8,128]{2,1,0:T(8,128)S(1)} %get-tuple-element.27), channel_id=1, source_target_pairs={{0,4},{1,5},{2,6},{3,7},{8,12},{9,13},{10,14},{11,15},{16,20},{17,... | collective-permute-start | bytes 221192 | tf_op jit(solution)/shard_map/ppermute | solution.py:400
  6.7 5.6 %collective-permute-start.1 = (f32[18,8,128]{2,1,0:T(8,128)S(1)}, f32[18,8,128]{2,1,0:T(8,128)S(1)}, u32[]{:S(2)}, u32[]{:S(2)}) collective-permute-start(f32[18,8,128]{2,1,0:T(8,128)S(1)} %get-tuple-element.28), channel_id=1, source_target_pairs={{4,8},{5,9},{6,10},{7,11},{12,16},{13,17},{14,18},{15,19},{20,24},... | collective-permute-start | bytes 221192 | tf_op jit(solution)/shard_map/ppermute | solution.py:400
  7.2 5.1 %collective-permute-start.4 = (f32[9,8,128]{2,1,0:T(8,128)S(1)}, f32[9,8,128]{2,1,0:T(8,128)S(1)}, u32[]{:S(2)}, u32[]{:S(2)}) collective-permute-start(f32[9,8,128]{2,1,0:T(8,128)S(1)} %get-tuple-element.32), channel_id=1, source_target_pairs={{4,8},{5,9},{6,10},{7,11},{12,16},{13,17},{14,18},{15,19},{20,24},... | collective-permute-start | bytes 110600 | tf_op jit(solution)/shard_map/ppermute | solution.py:409
  7.4 4.9 %collective-permute-start.5 = (f32[9,8,128]{2,1,0:T(8,128)S(1)}, f32[9,8,128]{2,1,0:T(8,128)S(1)}, u32[]{:S(2)}, u32[]{:S(2)}) collective-permute-start(f32[9,8,128]{2,1,0:T(8,128)S(1)} %get-tuple-element.33), channel_id=1, source_target_pairs={{0,4},{1,5},{2,6},{3,7},{8,12},{9,13},{10,14},{11,15},{16,20},{17,... | collective-permute-start | bytes 110600 | tf_op jit(solution)/shard_map/ppermute | solution.py:409

commit v4 on v3

--- a/solution.py
+++ b/solution.py
@@ -22,19 +22,28 @@
         self.u, self.s, self.wet = 0, levels, 2 * levels
         self.ce, self.cn, self.cot = 3 * levels, 3 * levels + 1, 3 * levels + 2
         self.count = 4 * levels + 2
-        self.parts = -(-self.count // 16)
-        self.strips = 2 * self.parts
+        self.parts, self.strips, self.paired = 2, 3, -(-levels // 2)
+        self.pair_at = self.cot - 16
+        assert 0 <= self.pair_at <= 8 - self.paired
+        self.place = {channel: (channel // 16, channel % 16) for channel in range(self.cot)}
+        self.place |= {self.cot + k: (1, self.pair_at + k // 2 + 8 * (k % 2)) for k in range(levels)}
         self.first = self.ce
         self.cot_at = self.strips + 2
-        self.second = self.cot_at + -(-levels // 2)
+        self.second = self.cot_at + self.paired
 
 
 def lane_iota(lanes):
     return lax.broadcasted_iota(jnp.int32, (TILE, lanes), 1)
 
 
-def shift_of(channel):
-    place = channel % 16
+def clear_halo(c, ref, rows):
+    zero = jnp.zeros((TILE, ref.shape[2]), jnp.float32)
+    for end in (pl.ds(0, TILE), pl.ds(HALO + rows, TILE)):
+        for channel in (*range(c.u, c.u + c.levels), *range(c.wet, c.wet + c.levels), c.cn):
+            ref[channel, end, :] = zero
+
+
+def shift_of(place):
     return 2 * DEPTH * (place % 8) + DEPTH * (place // 8)
 
 
@@ -44,10 +53,6 @@
 
 def is_odd(axis):
     return lax.rem(lax.axis_index(axis), 2) == 1
-
-
-def strip_rows(c, m):
-    return range(16 * m, min(16 * m + 16, c.count))
 
 
 def pack_kernel(
@@ -56,6 +61,7 @@
 ):
     levels = c.levels
     _, rows, lanes = u_ref.shape
+    own = pl.ds(HALO, rows)
     pieces = [(bottom_hbm, bottom_ref)]
     groups = [range(k, min(k + PIECE, levels)) for k in range(0, levels, PIECE)]
     for held in groups:
@@ -63,10 +69,11 @@
         pieces += [(land_hbm.at[at], land_ref.at[at]), (u_hbm.at[at], u_ref.at[at]), (s_hbm.at[at], s_ref.at[at])]
     pieces.append((c_hbm, c_ref))
     for held in groups:
-        pieces.append((a_hbm.at[pl.ds(held.start, len(held))], f_ref.at[pl.ds(c.cot + held.start, len(held))]))
+        pieces.append((a_hbm.at[pl.ds(held.start, len(held))], f_ref.at[pl.ds(c.cot + held.start, len(held)), own, :]))
     moves = [pltpu.make_async_copy(source, target, sems.at[i]) for i, (source, target) in enumerate(pieces)]
     for move in moves:
         move.start()
+    clear_halo(c, f_ref, rows)
     last_lat = lax.axis_index("lat") == lax.axis_size("lat") - 1
     moves[0].wait()
     for i, held in enumerate(groups):
@@ -74,14 +81,14 @@
             move.wait()
         for k in held:
             wet = jnp.where(k < bottom_ref[...], land_ref[k], 0).astype(jnp.float32)
-            f_ref[c.u + k] = wet * u_ref[k]
-            f_ref[c.s + k] = wet * s_ref[k]
-            f_ref[c.wet + k] = wet
+            f_ref[c.u + k, own, :] = wet * u_ref[k]
+            f_ref[c.s + k, own, :] = wet * s_ref[k]
+            f_ref[c.wet + k, own, :] = wet
     for move in moves[1 + 3 * len(groups) :]:
         move.wait()
-    f_ref[c.ce] = c_ref[0]
+    f_ref[c.ce, own, :] = c_ref[0]
     row = lax.broadcasted_iota(jnp.int32, (rows, lanes), 0)
-    f_ref[c.cn] = jnp.where(jnp.logical_and(last_lat, row == rows - 1), 0.0, c_ref[1])
+    f_ref[c.cn, own, :] = jnp.where(jnp.logical_and(last_lat, row == rows - 1), 0.0, c_ref[1])
     odd = is_odd("lon")
     group, groups = lane_iota(lanes) // DEPTH, lanes // DEPTH
     for t in range(rows // TILE):
@@ -89,9 +96,11 @@
         for m in range(c.parts):
             east = jnp.zeros((TILE, lanes), jnp.float32)
             west = east
-            for channel in strip_rows(c, m):
-                shift = shift_of(channel)
-                tile = f_ref[channel, at, :]
+            for channel, (part, place) in c.place.items():
+                if part != m:
+                    continue
+                shift = shift_of(place)
+                tile = f_ref[channel, pl.ds(HALO + t * TILE, TILE), :]
                 if shift:
                     tile = pltpu.roll(tile, shift, 1)
                 east = jnp.where(group == shift // DEPTH, tile, east)
@@ -100,35 +109,51 @@
             second_ref[m, at, :] = jnp.where(odd, west, east)
     odd_lat = is_odd("lat")
     for channel in range(c.first):
-        high, low = f_ref[channel, pl.ds(rows - TILE, TILE), :], f_ref[channel, pl.ds(0, TILE), :]
+        high, low = f_ref[channel, pl.ds(HALO + rows - TILE, TILE), :], f_ref[channel, pl.ds(HALO, TILE), :]
         lat_one_ref[channel] = jnp.where(odd_lat, low, high)
         lat_two_ref[channel] = jnp.where(odd_lat, high, low)
 
 
 def corner_kernel(c, f_ref, one_ref, two_ref, lat_one_ref, lat_two_ref):
     odd_lat, odd_lon = is_odd("lat"), is_odd("lon")
-    _, rows, lanes = f_ref.shape
+    _, rows, lanes = one_ref.shape
     half = TILE // 2
     first_half = lax.broadcasted_iota(jnp.int32, (TILE, lanes), 0) < half
-    low, high = pl.ds(0, TILE), pl.ds(rows - TILE, TILE)
-
-    def put(i, low_tile, high_tile):
-        lat_one_ref[i] = jnp.where(odd_lat, low_tile, high_tile)
-        lat_two_ref[i] = jnp.where(odd_lat, high_tile, low_tile)
-
-    for m in range(c.parts):
-        ends = [(one_ref[m, at, :], two_ref[m, at, :]) for at in (low, high)]
-        put(m, *(jnp.where(odd_lon, two, one) for one, two in ends))
-        put(c.parts + m, *(jnp.where(odd_lon, one, two) for one, two in ends))
+    lane = lane_iota(lanes)
+    pairs = 2 * DEPTH * c.pair_at - DEPTH
+    in_pairs = jnp.logical_and(lane >= pairs, lane < pairs + 2 * DEPTH * c.paired)
+    even_group = even_groups(lanes)
+
+    def two_levels(even, odd, high):
+        if high:
+            return jnp.where(first_half, pltpu.roll(even, half, 0), odd)
+        return jnp.where(first_half, even, pltpu.roll(odd, half, 0))
+
+    def put(i, low, high):
+        lat_one_ref[i] = jnp.where(odd_lat, low, high)
+        lat_two_ref[i] = jnp.where(odd_lat, high, low)
+
+    def strips(high):
+        at = pl.ds(rows - TILE if high else 0, TILE)
+        easts, wests = [], []
+        for m in range(c.parts):
+            one, two = one_ref[m, at, :], two_ref[m, at, :]
+            easts.append(jnp.where(odd_lon, two, one))
+            wests.append(jnp.where(odd_lon, one, two))
+        folded = [
+            jnp.where(in_pairs, two_levels(tile, pltpu.roll(tile, lanes - DEPTH, 1), high), tile)
+            for tile in (easts[1], wests[1])
+        ]
+        return easts[0], wests[0], jnp.where(even_group, *folded)
+
+    for i, (low, high) in enumerate(zip(strips(False), strips(True))):
+        put(i, low, high)
+    low, high = pl.ds(HALO, TILE), pl.ds(HALO + rows - TILE, TILE)
     put(c.strips, f_ref[c.ce, low, :], f_ref[c.ce, high, :])
     put(c.strips + 1, f_ref[c.cn, low, :], f_ref[c.cn, high, :])
-    for q in range(c.second - c.cot_at):
-        one, two = c.cot + 2 * q, c.cot + min(2 * q + 1, c.levels - 1)
-        put(
-            c.cot_at + q,
-            jnp.where(first_half, f_ref[one, low, :], pltpu.roll(f_ref[two, low, :], half, 0)),
-            jnp.where(first_half, pltpu.roll(f_ref[one, high, :], half, 0), f_ref[two, high, :]),
-        )
+    for q in range(c.paired):
+        even, odd = c.cot + 2 * q, c.cot + min(2 * q + 1, c.levels - 1)
+        put(c.cot_at + q, *(two_levels(f_ref[even, at, :], f_ref[odd, at, :], at is high) for at in (low, high)))
 
 
 class Sweeps:
@@ -148,15 +173,13 @@
         r0, r1 = pltpu.roll(x0, self.lanes - 1, 1), pltpu.roll(x1, self.lanes - 1, 1)
         return jnp.where(self.at_last, r1, r0), jnp.where(self.at_last, r0, r1)
 
-    def spread(self, row, easts, wests):
-        for m, (east, west) in enumerate(zip(easts, wests)):
-            both = jnp.where(self.even_group, east, west), jnp.where(self.even_group, west, east)
-            for channel in strip_rows(self.c, m):
-                shift = shift_of(channel)
-                tile = both[(channel % 16) // 8]
-                if shift:
-                    tile = pltpu.roll(tile, self.lanes - shift, 1)
-                self.e[1][channel, pl.ds(row, TILE), :] = tile
+    def mixed(self, east, west):
+        return jnp.where(self.even_group, east, west), jnp.where(self.even_group, west, east)
+
+    def ends(self, place, both):
+        shift = shift_of(place)
+        tile = both[place // 8]
+        return pltpu.roll(tile, self.lanes - shift, 1) if shift else tile
 
     def western(self, row):
         at = pl.ds(row, TILE)
@@ -249,27 +272,21 @@
             yield k, self.e[0][c.wet + k, at, :] * total
 
 
-def own_kernel(c, f_ref, one_ref, two_ref, e0, e1, w0, w1, d0, d1, x0, x1, m0, m1, adj, state, grad, gsource):
-    rows = f_ref.shape[1]
+def own_kernel(c, e0, one_ref, two_ref, e1, w0, w1, d0, d1, x0, x1, m0, m1, adj, state, grad, gsource):
+    rows, lanes = one_ref.shape[1:]
     odd_lon = is_odd("lon")
     s = Sweeps(c, (e0, e1), (w0, w1), (d0, d1), (x0, x1), (m0, m1), adj, state)
-    zero = jnp.zeros((TILE, f_ref.shape[2]), jnp.float32)
-    for ref in (e0, e1):
-        for end in (pl.ds(0, TILE), pl.ds(HALO + rows, TILE)):
-            for channel in (*range(c.u, c.u + c.levels), *range(c.wet, c.wet + c.levels), c.cn):
-                ref[channel, end, :] = zero
+    clear_halo(c, e1, rows)
     tiles = rows // TILE
     places = [HALO + t * TILE for t in range(tiles)]
     for t, row in enumerate(places):
         at, to = pl.ds(t * TILE, TILE), pl.ds(row, TILE)
-        for channel in range(c.count):
-            e0[channel, to, :] = f_ref[channel, at, :]
-        pairs = [(one_ref[m, at, :], two_ref[m, at, :]) for m in range(c.parts)]
-        s.spread(
-            row,
-            [jnp.where(odd_lon, two, one) for one, two in pairs],
-            [jnp.where(odd_lon, one, two) for one, two in pairs],
-        )
+        both = []
+        for m in range(c.parts):
+            one, two = one_ref[m, at, :], two_ref[m, at, :]
+            both.append(s.mixed(jnp.where(odd_lon, two, one), jnp.where(odd_lon, one, two)))
+        for channel, (part, place) in c.place.items():
+            e1[channel, to, :] = s.ends(place, both[part])
         s.western(row)
     s.over(s.diagonal, places, 1)
     for n in range(STEPS):
@@ -287,8 +304,6 @@
 def edge_kernel(
     c, first_one, first_two, second_two, second_one, *refs,
 ):
-    aliased = refs[: len(refs) // 2]
-    del aliased
     e0, e1, w0, w1, d0, d1, x0, x1, m0, m1, adj, state, grad, gsource, state_hbm, grad_hbm, gsource_hbm, sems = refs[14:]
     rows = grad.shape[1]
     s = Sweeps(c, (e0, e1), (w0, w1), (d0, d1), (x0, x1), (m0, m1), adj, state)
@@ -327,7 +342,15 @@
             if (k % 2 == 0) == low:
                 tile = pltpu.roll(tile, TILE // 2, 0)
             e0[c.cot + k, to, :] = tile
-        s.spread(row, second[: c.parts], second[c.parts : c.strips])
+        both = s.mixed(*second[:2]), (second[2],)
+        for channel in range(c.cot):
+            part, place = c.place[channel]
+            e1[channel, to, :] = s.ends(place, both[part])
+        for q in range(c.paired):
+            tile = s.ends(c.pair_at + q, both[1])
+            for k in range(2 * q, min(2 * q + 2, c.levels)):
+                moved = (k % 2 == 0) == low
+                e1[c.cot + k, to, :] = pltpu.roll(tile, TILE // 2, 0) if moved else tile
         s.western(row)
     top = lambda i: HALO + i - (DEPTH - 1)
     bottom = lambda i: HALO + rows - 1 - i
@@ -378,7 +401,7 @@
 
     fields, one, two, lat_one, lat_two = pl.pallas_call(
         functools.partial(pack_kernel, c),
-        out_shape=(f32(c.count, rows, lanes), *(f32(c.parts, rows, lanes),) * 2, *(f32(c.first, TILE, lanes),) * 2),
+        out_shape=(f32(c.count, span, lanes), *(f32(c.parts, rows, lanes),) * 2, *(f32(c.first, TILE, lanes),) * 2),
         in_specs=[hbm] * 6,
         out_specs=(vmem,) * 5,
         scratch_shapes=[
@@ -421,9 +444,9 @@
     )
     own = pl.pallas_call(
         functools.partial(own_kernel, c),
-        out_shape=shapes,
+        out_shape=shapes[1:],
         in_specs=[vmem] * 3,
-        out_specs=(vmem,) * len(shapes),
+        out_specs=(vmem,) * (len(shapes) - 1),
         compiler_params=params,
         cost_estimate=pl.CostEstimate(
             flops=2 * STEPS * levels * rows * lanes * 40, bytes_accessed=16 * 2**20, transcendentals=0
@@ -439,7 +462,7 @@
         scratch_shapes=[pltpu.SemaphoreType.DMA((9,))],
         compiler_params=params,
         name="edge_rows",
-    )(*first, *second[::-1], *own)
+    )(*first, *second[::-1], fields, *own)
     return tuple(out[len(shapes) :])
 
 

time: 14.3 us -> 14.3 us (level)
  transfers between devices with their start and end apart: 6 -> 6, of which waited for: 1 -> 1; matrix products, arithmetic and copies ran while one was open for 0% -> 0% of each run, Pallas kernels for 14% -> 15%
where the time goes in v4:
time: 14.3 us; the launch traced here: 14.1 us
  starting transfers between devices  7.66 us (54%)
  Pallas kernels  5.24 us (37%)
  between operations  0.68 us (5%)
  waiting for transfers between devices  0.51 us (4%)
    ppermute x2, starting transfers between devices, body(): lax.ppermute(lat_one, both, lat_pairs)  4.4 us
    ppermute x1, starting transfers between devices, body(): two = lax.ppermute(two, 'lon', swaps(lon, 1))  2.61 us
    pallas_call x1, Pallas kernels, body(): pl.pallas_call(functools.partial(own_kernel, c), out_shape=shapes[1:], in...  1.97 us
    pallas_call x1, Pallas kernels, body(): pl.pallas_call(functools.partial(edge_kernel, c), out_shape=(*shapes, *(f...  1.75 us
    pallas_call x1, Pallas kernels, body(): pl.pallas_call(functools.partial(pack_kernel, c), out_shape=(f32(c.count,...  1.44 us
    ppermute x1, starting transfers between devices, body(): one = lax.ppermute(one, 'lon', swaps(lon, 0))  0.52 us
    ppermute x1, waiting for transfers between devices, body(): two = lax.ppermute(two, 'lon', swaps(lon, 1))  0.49 us
  transfers between devices with their start and end apart: 6, of which 1 were waited for; matrix products, arithmetic and copies ran while one was open for 0% of the time, Pallas kernels for 15%

profile of v4, /device:TPU:0, one launch (start us, length us, event | category | flops | bytes accessed | tf_op | source)
XLA Modules:
  0.0 14.1 jit_solution(17222057651887135363)
XLA Ops:
  0.6 1.4 %pack.1 = (f32[26,64,128]{2,1,0:T(8,128)S(1)}, f32[2,48,128]{2,1,0:T(8,128)S(1)}, f32[2,48,128]{2,1,0:T(8,128)S(1)}, f32[18,8,128]{2,1,0:T(8,128)S(1)}, f32[18,8,128]{2,1,0:T(8,128)S(1)}) custom-call(f32[6,48,128]{2,1,0:T(8,128)} %u_hbm.1, f32[6,48,128]{2,1,0:T(8,128)} %s_hbm.1, f32[6,48,128]{2,1,0:T(8,128)} %a_hbm.1, f32[2,48,128]{2,1,0:T(8,128)} %c_hbm.1, ...), custom_call_target="tpu_custom_call" | custom-call | tf_op jit(solution)/shard_map/pack/pallas_call | solution.py:402
  2.1 0.5 %collective-permute-start.2 = (f32[2,48,128]{2,1,0:T(8,128)S(1)}, f32[2,48,128]{2,1,0:T(8,128)S(1)}, u32[]{:S(2)}, u32[]{:S(2)}) collective-permute-start(f32[2,48,128]{2,1,0:T(8,128)S(1)} %get-tuple-element.29), channel_id=1, source_target_pairs={{0,1},{2,3},{1,0},{3,2},{4,5},{6,7},{5,4},{7,6},{8,9},{10,11},{9,8... | collective-permute-start | bytes 147464 | tf_op jit(solution)/shard_map/ppermute | solution.py:419
  2.6 2.6 %collective-permute-start.3 = (f32[2,48,128]{2,1,0:T(8,128)S(1)}, f32[2,48,128]{2,1,0:T(8,128)S(1)}, u32[]{:S(2)}, u32[]{:S(2)}) collective-permute-start(f32[2,48,128]{2,1,0:T(8,128)S(1)} %get-tuple-element.30), channel_id=1, source_target_pairs={{1,2},{3,0},{2,1},{0,3},{5,6},{7,4},{6,5},{4,7},{9,10},{11,8},{10,... | collective-permute-start | bytes 147464 | tf_op jit(solution)/shard_map/ppermute | solution.py:420
  5.2 1.5 %collective-permute-start = (f32[18,8,128]{2,1,0:T(8,128)S(1)}, f32[18,8,128]{2,1,0:T(8,128)S(1)}, u32[]{:S(2)}, u32[]{:S(2)}) collective-permute-start(f32[18,8,128]{2,1,0:T(8,128)S(1)} %get-tuple-element.26), channel_id=1, source_target_pairs={{0,4},{1,5},{2,6},{3,7},{8,12},{9,13},{10,14},{11,15},{16,20},{17,... | collective-permute-start | bytes 221192 | tf_op jit(solution)/shard_map/ppermute | solution.py:423
  6.7 0.0 collective-permute-start.1
  6.7 0.0 collective-permute-done.2.one_ref
  6.7 0.5 %collective-permute-done.3.two_ref = f32[2,48,128]{2,1,0:T(8,128)S(1)} collective-permute-done((f32[2,48,128]{2,1,0:T(8,128)S(1)}, f32[2,48,128]{2,1,0:T(8,128)S(1)}, u32[]{:S(2)}, u32[]{:S(2)}) %collective-permute-start.3) | collective-permute-done | bytes 49184 | tf_op jit(solution)/shard_map/ppermute | solution.py:420
  7.2 0.1 corners.1
  7.3 0.1 collective-permute-start.4
  7.4 2.9 %collective-permute-start.5 = (f32[8,8,128]{2,1,0:T(8,128)S(1)}, f32[8,8,128]{2,1,0:T(8,128)S(1)}, u32[]{:S(2)}, u32[]{:S(2)}) collective-permute-start(f32[8,8,128]{2,1,0:T(8,128)S(1)} %get-tuple-element.32), channel_id=1, source_target_pairs={{0,4},{1,5},{2,6},{3,7},{8,12},{9,13},{10,14},{11,15},{16,20},{17,... | collective-permute-start | bytes 98312 | tf_op jit(solution)/shard_map/ppermute | solution.py:432
  10.3 2.0 %own_rows.1 = (f32[26,64,128]{2,1,0:T(8,128)S(1)}, f32[64,128]{1,0:T(8,128)S(1)}, f32[64,128]{1,0:T(8,128)S(1)}, f32[6,64,128]{2,1,0:T(8,128)S(1)}, f32[6,64,128...) custom-call(f32[26,64,128]{2,1,0:T(8,128)S(1)} %get-tuple-element.28, ...), custom_call_target="tpu_custom_call" | custom-call | flops 11796480 | bytes 16777216 | tf_op jit(solution)/shard_map/own_rows/pallas_call | solution.py:445
  12.3 0.0 collective-permute-done.first_one
  12.3 0.0 collective-permute-done.1.first_two
  12.3 0.0 collective-permute-done.4.second_two
  12.3 0.0 collective-permute-done.5.second_one
  12.3 1.7 %edge_rows.1 = (f32[26,64,128]{2,1,0:T(8,128)S(1)}, f32[26,64,128]{2,1,0:T(8,128)S(1)}, f32[64,128]{1,0:T(8,128)S(1)}, f32[64,128]{1,0:T(8,128)S(1)}, f32[6,64,1...) custom-call(f32[18,8,128]{2,1,0:T(8,128)S(1)} %collective-permute-do, ...), custom_call_target="tpu_custom_call", output_to_operand_aliasing={{0}: (4, {}), {1}: (5, {}), {2}: (6, {}), {3}: (7, {}), {4}... | custom-call | tf_op jit(solution)/shard_map/edge_rows/pallas_call | solution.py:456
Async XLA Ops:
  2.1 4.7 %collective-permute-start.2 = (f32[2,48,128]{2,1,0:T(8,128)S(1)}, f32[2,48,128]{2,1,0:T(8,128)S(1)}, u32[]{:S(2)}, u32[]{:S(2)}) collective-permute-start(f32[2,48,128]{2,1,0:T(8,128)S(1)} %get-tuple-element.29), channel_id=1, source_target_pairs={{0,1},{2,3},{1,0},{3,2},{4,5},{6,7},{5,4},{7,6},{8,9},{10,11},{9,8... | collective-permute-start | bytes 147464 | tf_op jit(solution)/shard_map/ppermute | solution.py:419
  2.6 4.6 %collective-permute-start.3 = (f32[2,48,128]{2,1,0:T(8,128)S(1)}, f32[2,48,128]{2,1,0:T(8,128)S(1)}, u32[]{:S(2)}, u32[]{:S(2)}) collective-permute-start(f32[2,48,128]{2,1,0:T(8,128)S(1)} %get-tuple-element.30), channel_id=1, source_target_pairs={{1,2},{3,0},{2,1},{0,3},{5,6},{7,4},{6,5},{4,7},{9,10},{11,8},{10,... | collective-permute-start | bytes 147464 | tf_op jit(solution)/shard_map/ppermute | solution.py:420
  5.2 7.1 %collective-permute-start = (f32[18,8,128]{2,1,0:T(8,128)S(1)}, f32[18,8,128]{2,1,0:T(8,128)S(1)}, u32[]{:S(2)}, u32[]{:S(2)}) collective-permute-start(f32[18,8,128]{2,1,0:T(8,128)S(1)} %get-tuple-element.26), channel_id=1, source_target_pairs={{0,4},{1,5},{2,6},{3,7},{8,12},{9,13},{10,14},{11,15},{16,20},{17,... | collective-permute-start | bytes 221192 | tf_op jit(solution)/shard_map/ppermute | solution.py:423
  6.7 5.6 %collective-permute-start.1 = (f32[18,8,128]{2,1,0:T(8,128)S(1)}, f32[18,8,128]{2,1,0:T(8,128)S(1)}, u32[]{:S(2)}, u32[]{:S(2)}) collective-permute-start(f32[18,8,128]{2,1,0:T(8,128)S(1)} %get-tuple-element.27), channel_id=1, source_target_pairs={{4,8},{5,9},{6,10},{7,11},{12,16},{13,17},{14,18},{15,19},{20,24},... | collective-permute-start | bytes 221192 | tf_op jit(solution)/shard_map/ppermute | solution.py:423
  7.3 5.0 %collective-permute-start.4 = (f32[8,8,128]{2,1,0:T(8,128)S(1)}, f32[8,8,128]{2,1,0:T(8,128)S(1)}, u32[]{:S(2)}, u32[]{:S(2)}) collective-permute-start(f32[8,8,128]{2,1,0:T(8,128)S(1)} %get-tuple-element.31), channel_id=1, source_target_pairs={{4,8},{5,9},{6,10},{7,11},{12,16},{13,17},{14,18},{15,19},{20,24},... | collective-permute-start | bytes 98312 | tf_op jit(solution)/shard_map/ppermute | solution.py:432
  7.4 4.9 %collective-permute-start.5 = (f32[8,8,128]{2,1,0:T(8,128)S(1)}, f32[8,8,128]{2,1,0:T(8,128)S(1)}, u32[]{:S(2)}, u32[]{:S(2)}) collective-permute-start(f32[8,8,128]{2,1,0:T(8,128)S(1)} %get-tuple-element.32), channel_id=1, source_target_pairs={{0,4},{1,5},{2,6},{3,7},{8,12},{9,13},{10,14},{11,15},{16,20},{17,... | collective-permute-start | bytes 98312 | tf_op jit(solution)/shard_map/ppermute | solution.py:432

commit v5 on v0

--- a/solution.py
+++ b/solution.py
@@ -271,7 +271,7 @@
 
 
 def edge_kernel(
-    c, first_one, first_two, second_two, second_one, *refs,
+    c, first_two, first_one, second_one, second_two, *refs,
 ):
     aliased = refs[: len(refs) // 2]
     del aliased
@@ -415,7 +415,7 @@
         scratch_shapes=[pltpu.SemaphoreType.DMA((3,))],
         compiler_params=params,
         name="edge_rows",
-    )(*first, *second[::-1], *own)
+    )(*first[::-1], *second, *own)
     return tuple(out[len(shapes) :])
 
 

time: 14.3 us -> 14.2 us (level)
  starting transfers between devices: 7.71 us -> 6.84 us
  waiting for transfers between devices: 0.51 us -> 1.32 us
    ppermute x2, waiting for transfers between devices: 0.01 us -> 1.31 us  [body(): lax.ppermute(lat_one, both, lat_pairs)]
    ppermute x2, starting transfers between devices: 4.4 us -> 3.48 us  [body(): lax.ppermute(lat_one, both, lat_pairs)]
    ppermute x1, waiting for transfers between devices: 0.49 us -> 0.01 us  [body(): two = lax.ppermute(two, 'lon', swaps(lon, 1))]
  transfers between devices with their start and end apart: 6 -> 6, of which waited for: 1 -> 2; matrix products, arithmetic and copies ran while one was open for 0% -> 0% of each run, Pallas kernels for 14% -> 15%
where the time goes in v5:
time: 14.2 us; the launch traced here: 14 us
  starting transfers between devices  6.84 us (48%)
  Pallas kernels  5.22 us (37%)
  waiting for transfers between devices  1.32 us (9%)
  between operations  0.67 us (5%)
    ppermute x2, starting transfers between devices, body(): lax.ppermute(lat_one, both, lat_pairs)  3.48 us
    ppermute x1, starting transfers between devices, body(): two = lax.ppermute(two, 'lon', swaps(lon, 1))  2.61 us
    pallas_call x1, Pallas kernels, body(): pl.pallas_call(functools.partial(own_kernel, c), out_shape=shapes, in_spe...  2.03 us
    pallas_call x1, Pallas kernels, body(): pl.pallas_call(functools.partial(edge_kernel, c), out_shape=(*shapes, *(f...  1.73 us
    pallas_call x1, Pallas kernels, body(): pl.pallas_call(functools.partial(pack_kernel, c), out_shape=(f32(c.count,...  1.44 us
    ppermute x2, waiting for transfers between devices, body(): lax.ppermute(lat_one, both, lat_pairs)  1.31 us
    ppermute x1, starting transfers between devices, body(): one = lax.ppermute(one, 'lon', swaps(lon, 0))  0.52 us
  transfers between devices with their start and end apart: 6, of which 2 were waited for; matrix products, arithmetic and copies ran while one was open for 0% of the time, Pallas kernels for 15%

profile of v5, /device:TPU:0, one launch (start us, length us, event | category | flops | bytes accessed | tf_op | source)
XLA Modules:
  0.0 14.0 jit_solution(769582338384451289)
XLA Ops:
  0.6 1.4 %pack.1 = (f32[26,48,128]{2,1,0:T(8,128)S(1)}, f32[2,48,128]{2,1,0:T(8,128)S(1)}, f32[2,48,128]{2,1,0:T(8,128)S(1)}, f32[18,8,128]{2,1,0:T(8,128)S(1)}, f32[18,8,128]{2,1,0:T(8,128)S(1)}) custom-call(f32[6,48,128]{2,1,0:T(8,128)} %u_hbm.1, f32[6,48,128]{2,1,0:T(8,128)} %s_hbm.1, f32[6,48,128]{2,1,0:T(8,128)} %a_hbm.1, f32[2,48,128]{2,1,0:T(8,128)} %c_hbm.1, ...), custom_call_target="tpu_custom_call" | custom-call | tf_op jit(solution)/shard_map/pack/pallas_call | solution.py:355
  2.1 0.5 %collective-permute-start.2 = (f32[2,48,128]{2,1,0:T(8,128)S(1)}, f32[2,48,128]{2,1,0:T(8,128)S(1)}, u32[]{:S(2)}, u32[]{:S(2)}) collective-permute-start(f32[2,48,128]{2,1,0:T(8,128)S(1)} %get-tuple-element.30), channel_id=1, source_target_pairs={{0,1},{2,3},{1,0},{3,2},{4,5},{6,7},{5,4},{7,6},{8,9},{10,11},{9,8... | collective-permute-start | bytes 147464 | tf_op jit(solution)/shard_map/ppermute | solution.py:372
  2.6 2.6 %collective-permute-start.3 = (f32[2,48,128]{2,1,0:T(8,128)S(1)}, f32[2,48,128]{2,1,0:T(8,128)S(1)}, u32[]{:S(2)}, u32[]{:S(2)}) collective-permute-start(f32[2,48,128]{2,1,0:T(8,128)S(1)} %get-tuple-element.31), channel_id=1, source_target_pairs={{1,2},{3,0},{2,1},{0,3},{5,6},{7,4},{6,5},{4,7},{9,10},{11,8},{10,... | collective-permute-start | bytes 147464 | tf_op jit(solution)/shard_map/ppermute | solution.py:373
  5.2 0.1 collective-permute-start
  5.3 3.0 %collective-permute-start.1 = (f32[18,8,128]{2,1,0:T(8,128)S(1)}, f32[18,8,128]{2,1,0:T(8,128)S(1)}, u32[]{:S(2)}, u32[]{:S(2)}) collective-permute-start(f32[18,8,128]{2,1,0:T(8,128)S(1)} %get-tuple-element.28), channel_id=1, source_target_pairs={{0,4},{1,5},{2,6},{3,7},{8,12},{9,13},{10,14},{11,15},{16,20},{17,... | collective-permute-start | bytes 221192 | tf_op jit(solution)/shard_map/ppermute | solution.py:376
  8.3 0.0 collective-permute-done.2.one_ref
  8.3 0.0 collective-permute-done.3.two_ref
  8.3 0.5 %collective-permute-start.4 = (f32[9,8,128]{2,1,0:T(8,128)S(1)}, f32[9,8,128]{2,1,0:T(8,128)S(1)}, u32[]{:S(2)}, u32[]{:S(2)}) collective-permute-start(f32[9,8,128]{2,1,0:T(8,128)S(1)} %get-tuple-element.32), channel_id=1, source_target_pairs={{0,4},{1,5},{2,6},{3,7},{8,12},{9,13},{10,14},{11,15},{16,20},{17,... | collective-permute-start | bytes 110600 | tf_op jit(solution)/shard_map/ppermute | solution.py:385
  8.8 0.2 %collective-permute-start.5 = (f32[9,8,128]{2,1,0:T(8,128)S(1)}, f32[9,8,128]{2,1,0:T(8,128)S(1)}, u32[]{:S(2)}, u32[]{:S(2)}) collective-permute-start(f32[9,8,128]{2,1,0:T(8,128)S(1)} %get-tuple-element.33), channel_id=1, source_target_pairs={{4,8},{5,9},{6,10},{7,11},{12,16},{13,17},{14,18},{15,19},{20,24},... | collective-permute-start | bytes 110600 | tf_op jit(solution)/shard_map/ppermute | solution.py:385
  9.0 2.0 %own_rows.1 = (f32[26,64,128]{2,1,0:T(8,128)S(1)}, f32[26,64,128]{2,1,0:T(8,128)S(1)}, f32[64,128]{1,0:T(8,128)S(1)}, f32[64,128]{1,0:T(8,128)S(1)}, f32[6,64,12...) custom-call(f32[26,48,128]{2,1,0:T(8,128)S(1)} %get-tuple-element.29, ...), custom_call_target="tpu_custom_call" | custom-call | flops 11796480 | bytes 16777216 | tf_op jit(solution)/shard_map/own_rows/pallas_call | solution.py:398
  11.0 0.0 collective-permute-done.first_two
  11.0 0.4 %collective-permute-done.1.first_one = f32[18,8,128]{2,1,0:T(8,128)S(1)} collective-permute-done((f32[18,8,128]{2,1,0:T(8,128)S(1)}, f32[18,8,128]{2,1,0:T(8,128)S(1)}, u32[]{:S(2)}, u32[]{:S(2)}) %collective-permute-start.1) | collective-permute-done | bytes 73760 | tf_op jit(solution)/shard_map/ppermute | solution.py:376
  11.4 0.9 %collective-permute-done.4.second_one = f32[9,8,128]{2,1,0:T(8,128)S(1)} collective-permute-done((f32[9,8,128]{2,1,0:T(8,128)S(1)}, f32[9,8,128]{2,1,0:T(8,128)S(1)}, u32[]{:S(2)}, u32[]{:S(2)}) %collective-permute-start.4) | collective-permute-done | bytes 36896 | tf_op jit(solution)/shard_map/ppermute | solution.py:385
  12.3 0.0 collective-permute-done.5.second_two
  12.3 1.7 %edge_rows.1 = (f32[26,64,128]{2,1,0:T(8,128)S(1)}, f32[26,64,128]{2,1,0:T(8,128)S(1)}, f32[64,128]{1,0:T(8,128)S(1)}, f32[64,128]{1,0:T(8,128)S(1)}, f32[6,64,1...) custom-call(f32[18,8,128]{2,1,0:T(8,128)S(1)} %collective-permute-do, ...), custom_call_target="tpu_custom_call", output_to_operand_aliasing={{0}: (4, {}), {1}: (5, {}), {2}: (6, {}), {3}: (7, {}), {4}... | custom-call | tf_op jit(solution)/shard_map/edge_rows/pallas_call | solution.py:409
  (1 shorter events, 0.0 us)
Async XLA Ops:
  2.1 6.2 %collective-permute-start.2 = (f32[2,48,128]{2,1,0:T(8,128)S(1)}, f32[2,48,128]{2,1,0:T(8,128)S(1)}, u32[]{:S(2)}, u32[]{:S(2)}) collective-permute-start(f32[2,48,128]{2,1,0:T(8,128)S(1)} %get-tuple-element.30), channel_id=1, source_target_pairs={{0,1},{2,3},{1,0},{3,2},{4,5},{6,7},{5,4},{7,6},{8,9},{10,11},{9,8... | collective-permute-start | bytes 147464 | tf_op jit(solution)/shard_map/ppermute | solution.py:372
  2.6 5.7 %collective-permute-start.3 = (f32[2,48,128]{2,1,0:T(8,128)S(1)}, f32[2,48,128]{2,1,0:T(8,128)S(1)}, u32[]{:S(2)}, u32[]{:S(2)}) collective-permute-start(f32[2,48,128]{2,1,0:T(8,128)S(1)} %get-tuple-element.31), channel_id=1, source_target_pairs={{1,2},{3,0},{2,1},{0,3},{5,6},{7,4},{6,5},{4,7},{9,10},{11,8},{10,... | collective-permute-start | bytes 147464 | tf_op jit(solution)/shard_map/ppermute | solution.py:373
  5.2 5.8 %collective-permute-start = (f32[18,8,128]{2,1,0:T(8,128)S(1)}, f32[18,8,128]{2,1,0:T(8,128)S(1)}, u32[]{:S(2)}, u32[]{:S(2)}) collective-permute-start(f32[18,8,128]{2,1,0:T(8,128)S(1)} %get-tuple-element.27), channel_id=1, source_target_pairs={{4,8},{5,9},{6,10},{7,11},{12,16},{13,17},{14,18},{15,19},{20,24},... | collective-permute-start | bytes 221192 | tf_op jit(solution)/shard_map/ppermute | solution.py:376
  5.3 6.1 %collective-permute-start.1 = (f32[18,8,128]{2,1,0:T(8,128)S(1)}, f32[18,8,128]{2,1,0:T(8,128)S(1)}, u32[]{:S(2)}, u32[]{:S(2)}) collective-permute-start(f32[18,8,128]{2,1,0:T(8,128)S(1)} %get-tuple-element.28), channel_id=1, source_target_pairs={{0,4},{1,5},{2,6},{3,7},{8,12},{9,13},{10,14},{11,15},{16,20},{17,... | collective-permute-start | bytes 221192 | tf_op jit(solution)/shard_map/ppermute | solution.py:376
  8.3 4.0 %collective-permute-start.4 = (f32[9,8,128]{2,1,0:T(8,128)S(1)}, f32[9,8,128]{2,1,0:T(8,128)S(1)}, u32[]{:S(2)}, u32[]{:S(2)}) collective-permute-start(f32[9,8,128]{2,1,0:T(8,128)S(1)} %get-tuple-element.32), channel_id=1, source_target_pairs={{0,4},{1,5},{2,6},{3,7},{8,12},{9,13},{10,14},{11,15},{16,20},{17,... | collective-permute-start | bytes 110600 | tf_op jit(solution)/shard_map/ppermute | solution.py:385
  8.8 3.5 %collective-permute-start.5 = (f32[9,8,128]{2,1,0:T(8,128)S(1)}, f32[9,8,128]{2,1,0:T(8,128)S(1)}, u32[]{:S(2)}, u32[]{:S(2)}) collective-permute-start(f32[9,8,128]{2,1,0:T(8,128)S(1)} %get-tuple-element.33), channel_id=1, source_target_pairs={{4,8},{5,9},{6,10},{7,11},{12,16},{13,17},{14,18},{15,19},{20,24},... | collective-permute-start | bytes 110600 | tf_op jit(solution)/shard_map/ppermute | solution.py:385
